TPU v7x, 128 devices: a whole 4x4x4 slice. The times are simulated.
128 devices in a mesh: tm: 4 (over z), space: 32 (over y, x, core).
Axes of the slice: x: 4, y: 4, z: 4, core: 2. Of those that a mesh axis runs over, the one named last changes fastest.
Arguments:
- latents: bfloat16 [8, 32, 120, 512], P('tm', 'space'), may hold values from -8 to 8
- spatial_weight: bfloat16 [4608, 512], replicated, may hold values from -0.09375 to 0.09375
- temporal_weight: bfloat16 [1536, 512], replicated, may hold values from -0.15625 to 0.15625
- qkv_weight: bfloat16 [512, 1536], replicated, may hold values from -0.25 to 0.25
- out_weight: bfloat16 [512, 512], replicated, may hold values from -0.25 to 0.25
- cotangent: bfloat16 [8, 32, 120, 512], P('tm', 'space'), may hold values from -6 to 6
Outputs:
- mixed: bfloat16 [8, 32, 120, 512], P('tm', 'space')
- grad_latents: bfloat16 [8, 32, 120, 512], P('tm', 'space')
- grad_weights: float32 [8192, 512], P(('tm', 'space'))
All inputs are finite; a program needn't handle non-finite values.
Results may differ from a plain program's by a relative error of at most 0.012.
The roundings to bfloat16 on the way count: a program that leaves them out, or rounds other values in their place, can miss the bound.
Values may be sent and summed in bfloat16 or wider, within the bound.
No kernel may reach another device: no remote copies, remote signals or barrier semaphores. Data moves between devices by JAX's collectives and lax.ppermute only.
A program may use at most 128 MiB of HBM per device.

v0:
```python
import functools
import math

import jax
import jax.numpy as jnp
from jax import lax
from jax.experimental import pallas as pl
from jax.experimental.pallas import tpu as pltpu
from jax.sharding import PartitionSpec as P

HEADS = 16
GROUP = 8
F32 = jnp.float32
BF = jnp.bfloat16
NT = (((1,), (1,)), ((), ()))

def dot_nt(left, right):
    return lax.dot_general(left, right, NT, preferred_element_type=F32)


def proj_kernel(x_ref, bext_ref, cot_ref, tw_ref, qw_ref, ow_ref, resid_ref, rres_ref, items_ref):
    frames, width, chans = x_ref.shape
    d = chans // HEADS
    for f in range(frames):
        acc = x_ref[f].astype(F32)
        for k in range(3):
            tap = tw_ref[k * chans : (k + 1) * chans, :]
            acc = acc + jnp.dot(bext_ref[f + k], tap, preferred_element_type=F32)
        resid_ref[f] = acc
        rounded = acc.astype(BF)
        rres_ref[f] = rounded
        qkv = jnp.dot(rounded, qw_ref[...], preferred_element_type=F32)
        dattn = dot_nt(cot_ref[f], ow_ref[...])
        for h in range(HEADS):
            parts = [qkv[:, p * chans + h * d : p * chans + (h + 1) * d] for p in range(3)]
            parts.append(dattn[:, h * d : (h + 1) * d])
            items_ref[f, h] = jnp.concatenate(parts, axis=1).astype(BF)


def proj(x, bext, cot, tw, qw, ow):
    frames, width, chans = x.shape
    return pl.pallas_call(
        proj_kernel,
        out_shape=(
            jax.ShapeDtypeStruct((frames, width, chans), F32),
            jax.ShapeDtypeStruct((frames, width, chans), BF),
            jax.ShapeDtypeStruct((frames, HEADS, width, 4 * chans // HEADS), BF),
        ),
        compiler_params=pltpu.CompilerParams(vmem_limit_bytes=32 << 20),
        cost_estimate=pl.CostEstimate(flops=10**9 * 2, bytes_accessed=6 << 20, transcendentals=0),
    )(x, bext, cot, tw, qw, ow)


def post_kernel(core_ref, z_ref, cot_ref, qw_ref, attn_ref, dres_ref, dresb_ref, mine_ref, other_ref):
    frames, width, chans = cot_ref.shape
    d = chans // HEADS
    half = chans // 2
    all_parts = []
    for f in range(frames):
        heads = [z_ref[f, h].astype(F32) for h in range(HEADS)]
        dres = cot_ref[f].astype(F32)
        parts = [jnp.concatenate([z[:, p * d : (p + 1) * d] for z in heads], axis=1).astype(BF) for p in range(4)]
        attn_ref[f] = parts[0]
        for p in range(3):
            dres = dres + dot_nt(parts[p + 1], qw_ref[:, p * chans : (p + 1) * chans])
        dres_ref[f] = dres
        dresb = dres.astype(BF)
        dresb_ref[f] = dresb
        all_parts.append(parts[1:] + [dresb])

    def store(first, second):
        for f in range(frames):
            for at, part in enumerate(all_parts[f]):
                for out, c in ((first, 0), (second, 1)):
                    out[f, :, at * half : (at + 1) * half] = part[:, c * half : (c + 1) * half]

    @pl.when(core_ref[0] == 0)
    def _():
        store(mine_ref, other_ref)

    @pl.when(core_ref[0] == 1)
    def _():
        store(other_ref, mine_ref)


def post(core, z, cot, qw):
    frames, width, chans = cot.shape
    return pl.pallas_call(
        post_kernel,
        out_shape=(
            jax.ShapeDtypeStruct((frames, width, chans), BF),
            jax.ShapeDtypeStruct((frames, width, chans), F32),
            jax.ShapeDtypeStruct((frames, width, chans), BF),
            jax.ShapeDtypeStruct((frames, width, 2 * chans), BF),
            jax.ShapeDtypeStruct((frames, width, 2 * chans), BF),
        ),
        in_specs=[pl.BlockSpec(memory_space=pltpu.SMEM)] + [pl.BlockSpec(memory_space=pltpu.VMEM)] * 3,
        compiler_params=pltpu.CompilerParams(vmem_limit_bytes=32 << 20),
        cost_estimate=pl.CostEstimate(flops=10**9, bytes_accessed=6 << 20, transcendentals=0),
    )(core, z, cot, qw)


def fetch_kernel(w_ref, out_ref):
    out_ref[...] = w_ref[...]


def fetch(w):
    return pl.pallas_call(
        fetch_kernel,
        out_shape=jax.ShapeDtypeStruct(w.shape, w.dtype),
        compiler_params=pltpu.CompilerParams(vmem_limit_bytes=24 << 20),
        cost_estimate=pl.CostEstimate(flops=10**6, bytes_accessed=10 << 20, transcendentals=0),
    )(w)


def attn_kernel(scale, tq, ck, un, x_ref, o_ref, a_ref, kt_ref, vt_ref, s_ref, e_ref, acc_ref):
    tok = x_ref.shape[0]
    step = pl.program_id(0)
    nck = tok // ck
    d = 32
    @pl.when(step == 0)
    def _():
        k = x_ref[:, d:2*d]
        v = x_ref[:, 2*d:3*d]
        lane = lax.broadcasted_iota(jnp.int32, (tok, d), 1)
        ones = jnp.where(lane < 3, 1.0, 0.0).astype(BF)
        a_ref[...] = jnp.concatenate([k, k, v, ones], axis=1)
        kt_ref[...] = k.astype(F32).T.astype(BF)
        vt_ref[...] = jnp.concatenate([v, ones], axis=1).astype(F32).T[: d + 16].astype(BF)
        acc_ref[...] = jnp.zeros_like(acc_ref)
    rows = pl.ds(pl.multiple_of(step * tq, tq), tq)
    xb = x_ref[rows, :]
    q = xb[:, 0:d].astype(F32)
    do = xb[:, 3*d:4*d].astype(F32)
    zeros = jnp.zeros((tq, 2*d), BF)
    def split(z):
        hi = z.astype(BF)
        lo = (z - hi.astype(F32)).astype(BF)
        return hi, lo
    qh, ql = split(q * (scale * math.log2(math.e)))
    wq = jnp.concatenate([qh, ql, zeros], axis=1)
    def p1(i, m):
        r = pl.ds(pl.multiple_of(i * ck, ck), ck)
        s = lax.dot_general(a_ref[r, :], wq, NT, preferred_element_type=F32)
        s_ref[r, :] = s
        return jnp.maximum(m, jnp.max(s.reshape(ck // 8, 8, tq), axis=0))
    m = lax.fori_loop(0, nck, p1, jnp.full((8, tq), -jnp.inf, F32), unroll=un)
    m = jnp.max(m, axis=0, keepdims=True)
    def p2(i, o):
        r = pl.ds(pl.multiple_of(i * ck, ck), ck)
        e = jnp.exp2(s_ref[r, :] - m)
        s_ref[r, :] = e
        eb = e.astype(BF)
        e_ref[r, :] = eb
        return o + jnp.dot(vt_ref[:, r], eb, preferred_element_type=F32)
    o = lax.fori_loop(0, nck, p2, jnp.zeros((d + 16, tq), F32), unroll=un)
    inv = 1.0 / o[d:d+1, :]
    ot = o[:d] * inv
    ob = ot.T
    delta = jnp.sum(ob * do, axis=1, keepdims=True)
    invc = jnp.broadcast_to(inv, (8, tq)).T[:, 0:1]
    dh = (-delta).astype(BF); dr = -delta - dh.astype(F32)
    dm = dr.astype(BF); dl = (dr - dm.astype(F32)).astype(BF)
    lane = lax.broadcasted_iota(jnp.int32, (tq, d), 1)
    dd = jnp.where(lane == 0, dh.astype(F32), jnp.where(lane == 1, dm.astype(F32), jnp.where(lane == 2, dl.astype(F32), 0.0))).astype(BF)
    wd = jnp.concatenate([zeros, xb[:, 3*d:], dd], axis=1)
    gh, gl = split(do * invc)
    rh, rl = split(q * (invc * scale))
    none = zeros[:, :d]
    we = jnp.concatenate([none, gl, none, gh], axis=1)
    ws = jnp.concatenate([rl, none, rh, none], axis=1)
    def p3(i, dq):
        r = pl.ds(pl.multiple_of(i * ck, ck), ck)
        dp = lax.dot_general(a_ref[r, :], wd, NT, preferred_element_type=F32)
        ds = (s_ref[r, :] * dp).astype(BF)
        acc_ref[r, :] += (jnp.dot(ds, ws, preferred_element_type=F32)
                          + jnp.dot(e_ref[r, :], we, preferred_element_type=F32))
        return dq + jnp.dot(kt_ref[:, r], ds, preferred_element_type=F32)
    dq = lax.fori_loop(0, nck, p3, jnp.zeros((d, tq), F32), unroll=un)
    dq = dq * (inv * scale)
    o_ref[rows, 0:2*d] = jnp.concatenate([ot, dq], axis=0).T.astype(BF)
    @pl.when(step == pl.num_programs(0) - 1)
    def _():
        acc = acc_ref[...]
        acc = acc + pltpu.roll(acc, 2*d, 1)
        o_ref[:, 2*d:] = acc[:, 2*d:].astype(BF)

def attn(x, tq=768, ck=3840, un=1):
    tok = x.shape[0]
    return pl.pallas_call(
        functools.partial(attn_kernel, 1.0/math.sqrt(32), tq, ck, un),
        grid=(tok // tq,),
        in_specs=[pl.BlockSpec((tok, 128), lambda i: (0, 0))],
        out_specs=pl.BlockSpec((tok, 128), lambda i: (0, 0)),
        out_shape=jax.ShapeDtypeStruct((tok, 128), BF),
        scratch_shapes=[pltpu.VMEM((tok, 128), BF), pltpu.VMEM((32, tok), BF), pltpu.VMEM((48, tok), BF),
                        pltpu.VMEM((tok, tq), F32), pltpu.VMEM((tok, tq), BF), pltpu.VMEM((tok, 128), F32)],
        compiler_params=pltpu.CompilerParams(vmem_limit_bytes=48 << 20),
        cost_estimate=pl.CostEstimate(flops=6*2*tok*tok*128, bytes_accessed=4*tok*128, transcendentals=tok*tok),
    )(x)


LANES = 128
CALL = functools.partial(pltpu.CompilerParams, vmem_limit_bytes=40 << 20)


def cost(flops, moved):
    return pl.CostEstimate(flops=int(flops), bytes_accessed=int(moved), transcendentals=0)


def padded(plane):
    width, chans = plane.shape
    return jnp.concatenate([plane.astype(F32), jnp.zeros((LANES - width, chans), F32)], axis=0)


def pick_kernel(rows, act_ref, outer_ref, out_ref):
    group = out_ref.shape[0]
    frames, width, chans = act_ref.shape
    for f in range(frames):
        for at, src in ((f, act_ref), (frames + f, outer_ref)):
            plane = src[f].astype(F32)
            for c in range(2):
                parts = [plane[:, b + c * rows : b + (c + 1) * rows] for b in range(0, chans, 2 * rows)]
                part = jnp.concatenate(parts, axis=1).astype(BF)
                for x in range(group // 2):
                    out_ref[2 * x + c, at] = part


def pick(act, outer, rows):
    frames, width, chans = act.shape
    return pl.pallas_call(
        functools.partial(pick_kernel, rows),
        out_shape=jax.ShapeDtypeStruct((GROUP, 2 * frames, width, chans // 2), BF),
        compiler_params=CALL(),
        cost_estimate=cost(1e8, 3 << 20),
    )(act, outer)


def turn_kernel(r_ref, at_ref):
    group = r_ref.shape[0]
    frames = at_ref.shape[1]
    for f in range(frames):
        for row in range(group + 2):
            if row == 0:
                plane = r_ref[0, frames + f]
            elif row == group + 1:
                plane = r_ref[group - 1, frames + f]
            else:
                plane = r_ref[row - 1, f]
            tile = padded(plane).T
            cols = slice(row * LANES, (row + 1) * LANES)
            at_ref[0, f, :, cols] = pltpu.roll(tile, 1, 1).astype(BF)
            at_ref[1, f, :, cols] = tile.astype(BF)
            at_ref[2, f, :, cols] = pltpu.roll(tile, LANES - 1, 1).astype(BF)


def turn(r, frames):
    group, _, _, chans = r.shape
    return pl.pallas_call(
        turn_kernel,
        out_shape=jax.ShapeDtypeStruct((3, frames, chans, (group + 2) * LANES), BF),
        compiler_params=CALL(),
        cost_estimate=cost(1e9, 6 << 20),
    )(r)


def turn_pair_kernel(*refs):
    ins, outs = refs[:4], refs[4:]
    for own, other, out in ((ins[0], ins[1], outs[0]), (ins[2], ins[3], outs[1])):
        count = own.shape[0]
        for d, src in enumerate((own, other)):
            for f in range(count):
                at = (d * count + f) * LANES
                out[:, at : at + LANES] = padded(src[f]).T.astype(BF)


def turn_pair(own_r, other_r, own_b, other_b):
    chans = own_r.shape[-1]
    return pl.pallas_call(
        turn_pair_kernel,
        out_shape=tuple(
            jax.ShapeDtypeStruct((chans, 2 * x.shape[0] * LANES), BF) for x in (own_r, own_b)
        ),
        compiler_params=CALL(),
        cost_estimate=cost(1e9, 4 << 20),
    )(own_r, other_r, own_b, other_b)


def local_terms_kernel(
    line_ref, rt_ref, bt_ref, a0_ref, a1_ref, p0_ref, p1_ref, c0_ref, c1_ref, *refs
):
    outs, (at_ref, pay_ref, cot_ref, mix_ref, out_ref) = refs[:4], refs[4:]
    frames, width, chans = a0_ref.shape
    half = chans // 2
    for d, (a, p, c) in enumerate(((a0_ref, p0_ref, c0_ref), (a1_ref, p1_ref, c1_ref))):
        for f in range(frames):
            at = (d * frames + f) * LANES
            at_ref[:, at : at + LANES] = padded(a[f]).T.astype(BF)
            pay_ref[at : at + LANES, :] = padded(p[f]).astype(BF)
            cot_ref[at : at + LANES, :] = padded(c[f]).astype(BF)
    parts, _, rows, _ = out_ref.shape
    block = parts * rows

    def put(first, value, lane=0):
        for n in range(value.shape[0] // block):
            for y in range(parts):
                at = n * block + y * rows
                out_ref[y, first + n, :, lane : lane + value.shape[1]] = value[at : at + rows].astype(BF)

    for k in range(3):
        acc = jnp.zeros((chans, half), F32)
        for d in range(2):
            left = bt_ref[:, (2 * d * frames + k) * LANES : (2 * d * frames + k + frames) * LANES]
            right = pay_ref[d * frames * LANES : (d + 1) * frames * LANES, 3 * half :]
            acc = acc + jnp.dot(left, right, preferred_element_type=F32)
        put(k * chans // block, acc)
    for p in range(3):
        right = pay_ref[:, p * half : (p + 1) * half]
        for lane in range(0, half, LANES):
            value = jnp.dot(rt_ref[...], right[:, lane : lane + LANES], preferred_element_type=F32)
            mix_ref[lane // LANES, pl.ds(p, chans, stride=3), :] = value
    for lane in range(0, half, LANES):
        put(3 * chans // block, mix_ref[lane // LANES], lane)
    put(6 * chans // block, jnp.dot(at_ref[...], cot_ref[...], preferred_element_type=F32))
    for k, out in enumerate(outs):
        out[...] = out_ref[lax.rem(line_ref[0] + k, parts)]


def local_terms(line, rt, bt, atted, pay, cot):
    frames, width, chans = atted[0].shape
    half = chans // 2
    span = 2 * frames * LANES
    piece = (7 * chans // 64, 16, half)
    return pl.pallas_call(
        local_terms_kernel,
        out_shape=(jax.ShapeDtypeStruct(piece, BF),) * 4,
        in_specs=[pl.BlockSpec(memory_space=pltpu.SMEM)] + [pl.BlockSpec(memory_space=pltpu.VMEM)] * 8,
        scratch_shapes=[
            pltpu.VMEM((chans, span), BF),
            pltpu.VMEM((span, 4 * half), BF),
            pltpu.VMEM((span, half), BF),
            pltpu.VMEM((half // LANES, 3 * chans, LANES), F32),
            pltpu.VMEM((4,) + piece, BF),
        ],
        compiler_params=CALL(),
        cost_estimate=cost(2e9, 10 << 20),
    )(line, rt, bt, *atted, *pay, *cot)


def conv_terms_kernel(at_ref, dpre_ref, *refs):
    parts, (out_ref, dp_ref, acc_ref, part_ref, sems) = refs[:4], refs[4:]
    step = pl.program_id(0)
    group, _, width, cols = dpre_ref.shape
    shifts, _, chans, _ = at_ref.shape
    rows = out_ref.shape[1]
    blocks = chans // rows
    copies = [pltpu.make_async_copy(src, part_ref.at[k], sems.at[k]) for k, src in enumerate(parts)]

    @pl.when(step == 0)
    def _():
        for copy in copies:
            copy.start()

    for row in range(group):
        dp_ref[row * LANES : (row + 1) * LANES, :] = padded(dpre_ref[row, 0]).astype(BF)
    span = group * LANES

    def product(i):
        left = at_ref[:, 0, :, i * LANES : i * LANES + span].reshape(shifts * chans, span)
        return jnp.dot(left, dp_ref[...], preferred_element_type=F32)

    @pl.when(step == 0)
    def _():
        for i in range(3):
            acc_ref[i] = product(i)

    @pl.when(step == 1)
    def _():
        for i in range(3):
            value = (acc_ref[i] + product(i)).astype(BF)
            for b in range(shifts * blocks):
                out_ref[i * shifts * blocks + b] = value[b * rows : (b + 1) * rows]
        for copy in copies:
            copy.wait()
        for n in range(part_ref.shape[1]):
            value = part_ref[0, n].astype(F32)
            for k in range(1, 4):
                value = value + part_ref[k, n].astype(F32)
            value = value.astype(BF)
            out_ref[3 * shifts * blocks + n] = jnp.concatenate([value[:, :cols], value[:, cols:]], axis=0)


def conv_terms(at, dpre, parts, owners, rows):
    group, frames, width, cols = dpre.shape
    shifts, _, chans, lanes = at.shape
    assert frames == 2
    return pl.pallas_call(
        conv_terms_kernel,
        grid=(frames,),
        in_specs=[
            pl.BlockSpec((shifts, 1, chans, lanes), lambda f: (0, f, 0, 0)),
            pl.BlockSpec((group, 1, width, cols), lambda f: (0, f, 0, 0)),
        ]
        + [pl.BlockSpec(memory_space=pl.ANY)] * 4,
        out_specs=pl.BlockSpec((owners, rows, cols), lambda f: (0, 0, 0)),
        out_shape=jax.ShapeDtypeStruct((owners, rows, cols), BF),
        scratch_shapes=[
            pltpu.VMEM((group * LANES, cols), BF),
            pltpu.VMEM((3, shifts * chans, cols), F32),
            pltpu.VMEM((4,) + parts[0].shape, BF),
            pltpu.SemaphoreType.DMA((4,)),
        ],
        compiler_params=pltpu.CompilerParams(vmem_limit_bytes=60 << 20),
        cost_estimate=cost(2e9, 10 << 20),
    )(at, dpre, *parts)


def sum_kernel(norm, dims, which_ref, terms_ref, out_ref):
    times, ys, xs = dims
    rows, cols = terms_ref.shape[1:]

    @pl.when(which_ref[0] == 1)
    def _():
        for x in range(xs):
            for c in range(2):
                acc = jnp.zeros((rows, cols), F32)
                for t in range(times):
                    for y in range(ys):
                        acc = acc + terms_ref[((t * ys + y) * xs + x) * 2 + c].astype(F32)
                out_ref[c * rows : (c + 1) * rows, x * cols : (x + 1) * cols] = acc * norm

    @pl.when(which_ref[0] == 0)
    def _():
        part = rows // 2
        for y in range(ys):
            for c in range(2):
                acc = jnp.zeros((rows, cols), F32)
                for t in range(times):
                    for x in range(xs):
                        acc = acc + terms_ref[((t * ys + y) * xs + x) * 2 + c].astype(F32)
                acc = acc * norm
                for h in range(2):
                    at = (2 * c + h) * cols
                    out_ref[y * part : (y + 1) * part, at : at + cols] = acc[h * part : (h + 1) * part]


def sum_terms(which, terms, norm, dims):
    owners, rows, cols = terms.shape
    return pl.pallas_call(
        functools.partial(sum_kernel, norm, dims),
        out_shape=jax.ShapeDtypeStruct((2 * rows, 4 * cols), F32),
        in_specs=[pl.BlockSpec(memory_space=pltpu.SMEM), pl.BlockSpec(memory_space=pltpu.VMEM)],
        compiler_params=CALL(),
        cost_estimate=cost(1e7, 1 << 20),
    )(which, terms)


def dpre_kernel(own_ref, next_ref, slope_ref, tw_ref, dpre_ref, near_ref):
    frames, width, chans = own_ref.shape
    group, _, _, cols = near_ref.shape
    ext = [own_ref[f] for f in range(frames)] + [next_ref[f] for f in range(frames)]
    for f in range(frames):
        acc = jnp.zeros((width, chans), F32)
        for k in range(3):
            acc = acc + dot_nt(ext[f + 2 - k], tw_ref[k * chans : (k + 1) * chans, :])
        value = (acc * slope_ref[f]).astype(BF)
        dpre_ref[f] = value
        for e in range(group):
            near_ref[e, f] = value[:, (e // 2) * cols : (e // 2 + 1) * cols]


def make_dpre(own, nxt, slope, tw):
    frames, width, chans = own.shape
    return pl.pallas_call(
        dpre_kernel,
        out_shape=(
            jax.ShapeDtypeStruct((frames, width, chans), BF),
            jax.ShapeDtypeStruct((GROUP, frames, width, 2 * chans // GROUP), BF),
        ),
        compiler_params=CALL(),
        cost_estimate=cost(5e8, 3 << 20),
    )(own, nxt, slope, tw)


def dact_kernel(mid_ref, above_ref, below_ref, dres_ref, x_ref, sw_ref, out_ref):
    frames, width, chans = mid_ref.shape
    line = lax.broadcasted_iota(jnp.int32, (width, chans), 0)
    for f in range(frames):
        acc = jnp.zeros((width, chans), F32)
        for i, src in enumerate((below_ref, mid_ref, above_ref)):
            plane = src[f]
            wide = plane.astype(F32)
            right = jnp.where(line == width - 1, 0.0, pltpu.roll(wide, width - 1, 0)).astype(BF)
            left = jnp.where(line == 0, 0.0, pltpu.roll(wide, 1, 0)).astype(BF)
            for j, value in enumerate((right, plane, left)):
                tap = 3 * i + j
                acc = acc + dot_nt(value, sw_ref[tap * chans : (tap + 1) * chans, :])
        x = x_ref[f].astype(F32)
        sigma = 1.0 / (1.0 + jnp.exp(-x))
        slope = sigma * (1.0 + x * (1.0 - sigma))
        out_ref[f] = (dres_ref[f] + acc * slope).astype(BF)


def make_grad_latents(mid, above, below, dres, x, sw):
    return pl.pallas_call(
        dact_kernel,
        out_shape=jax.ShapeDtypeStruct(mid.shape, BF),
        compiler_params=CALL(),
        cost_estimate=cost(2e9, 8 << 20),
    )(mid, above, below, dres, x, sw)


def silu_slope(value):
    sigma = jax.nn.sigmoid(value)
    return sigma * (1.0 + value * (1.0 - sigma))


def matmul(left, right):
    return jnp.dot(left, right, preferred_element_type=F32)


def shift(x, axis, by):
    count = lax.axis_size(axis)
    pairs = [(i, i + by) for i in range(count) if 0 <= i + by < count]
    return lax.ppermute(x, axis, pairs)


def swap(x):
    count = lax.axis_size("space")
    return lax.ppermute(x, "space", [(i, i ^ 1) for i in range(count)])


def neighbours(field):
    return shift(field, "space", 1), shift(field, "space", -1)


def exchange(x):
    count = lax.axis_size("space")
    groups = [list(range(at, at + GROUP)) for at in range(0, count, GROUP)]
    return lax.all_to_all(x, "space", 0, 0, axis_index_groups=groups, tiled=True)


def along_y(x, by):
    count = lax.axis_size("space")
    return lax.ppermute(x, "space", [(i, (i + by * GROUP) % count) for i in range(count)])


def pick_one(x, index):
    return lax.dynamic_index_in_dim(x, index, 0, keepdims=False)


def side_pad(field):
    return jnp.pad(field, ((0, 0), (0, 0), (1, 1), (0, 0)))


def taps_of(padded, width):
    pieces = [padded[:, i, j : j + width] for i in range(3) for j in range(3)]
    return jnp.concatenate(pieces, axis=-1).reshape(-1, 9 * padded.shape[-1])


def per_device(latents, spatial_weight, temporal_weight, qkv_weight, out_weight, cotangent):
    frames, rows, width, chans = latents.shape
    ntok = frames * width
    n_space = lax.axis_size("space")
    n_time = lax.axis_size("tm")
    owners = n_space * n_time
    depth = chans // HEADS
    norm = 1.0 / math.sqrt(ntok * n_space * n_time)
    here = lax.axis_index("space")
    core, line = here % 2, here // GROUP
    half = chans // 2
    share = 16 * chans // (2 * owners)

    x = latents.reshape(frames, width, chans)
    cot = cotangent.reshape(frames, width, chans)
    act = jax.nn.silu(x.astype(F32)).astype(BF)
    above, below = neighbours(act)
    pre = matmul(taps_of(side_pad(jnp.stack([above, act, below], axis=1)), width), fetch(spatial_weight))
    pre = pre.reshape(frames, width, chans)
    bact = jax.nn.silu(pre).astype(BF)
    bext = jnp.concatenate([shift(bact, "tm", 1), bact], axis=0)
    resid, rres, items = proj(x, bext, cot, temporal_weight, qkv_weight, out_weight)
    items = items.reshape(frames * HEADS, width, 4 * depth)
    items = lax.all_to_all(items, "space", 0, 0, tiled=True)

    early = pick(act, jnp.where(here % GROUP == 0, above, below), share)
    chalf = cot.reshape(frames, width, 2, half).transpose(2, 0, 1, 3)
    cpair = (pick_one(chalf, core), swap(pick_one(chalf, 1 - core)))
    rother, bother = swap(rres), swap(bext)
    early, cpair, rother, bother, items = lax.optimization_barrier((early, cpair, rother, bother, items))
    early = exchange(early)
    outs = attn(items.reshape(n_space * width, 4 * depth)).reshape(n_space, width, 4 * depth)
    outs, early, rother, bother = lax.optimization_barrier((outs, early, rother, bother))
    outs = lax.all_to_all(outs, "space", 0, 0, tiled=True)
    aturn = turn(early, frames)
    rturn, bturn = turn_pair(rres, rother, bext, bother)
    slope = silu_slope(pre)
    outs, aturn, rturn, bturn, slope = lax.optimization_barrier((outs, aturn, rturn, bturn, slope))

    core_at = core.astype(jnp.int32).reshape(1)
    outs = outs.reshape(frames, HEADS, width, 4 * depth)
    atted, dres, dresb, mine, other = post(core_at, outs, cot, qkv_weight)
    dnext = shift(dresb, "tm", -1)
    local = local_terms(line.astype(jnp.int32).reshape(1), rturn, bturn, (atted, swap(atted)), (mine, swap(other)), cpair)
    slope, _ = lax.optimization_barrier((slope, local[0]))
    dpre, near = make_dpre(dresb, dnext, slope, temporal_weight)
    near = exchange(near)
    dabove, dbelow = neighbours(dpre)
    parts = [local[0]] + [along_y(local[by], by) for by in range(1, 4)]
    mixed = resid.reshape(ntok, chans) + matmul(atted.reshape(ntok, chans), out_weight)
    mixed = mixed.astype(BF).reshape(latents.shape)
    mixed, near = lax.optimization_barrier((mixed, near))
    terms = conv_terms(aturn, near, parts, owners, share)
    terms, dpre, dabove, dbelow = lax.optimization_barrier((terms, dpre, dabove, dbelow))
    terms = lax.all_to_all(terms, ("tm", "space"), 0, 0, tiled=True)
    grad_latents = make_grad_latents(dpre, dabove, dbelow, dres, x, spatial_weight).reshape(latents.shape)
    index = lax.axis_index("tm") * n_space + here
    which = (index < 9 * chans // (2 * share)).astype(jnp.int32).reshape(1)
    grad_weights = sum_terms(which, terms, norm, (n_time, n_space // GROUP, GROUP // 2))
    return (mixed, grad_latents, grad_weights)


def solution(mesh):
    placed = (P("tm", "space", None, None), P(), P(), P(), P(), P("tm", "space", None, None))
    return jax.shard_map(
        per_device,
        mesh=mesh,
        in_specs=placed,
        out_specs=(
            P("tm", "space", None, None),
            P("tm", "space", None, None),
            P(("tm", "space"), None),
        ),
        check_vma=False,
    )
```

profile of v0, /device:TPU:1, one launch (start us, length us, event | category | flops | bytes accessed | tf_op | source)
XLA Modules:
  0.0 200.1 jit_solution(11595661237114641896)
XLA Ops:
  1.7 3.3 %collective-permute-start.1 = (bf16[2,120,512]{2,1,0:T(8,128)(2,1)S(1)}, bf16[2,120,512]{2,1,0:T(8,128)(2,1)S(1)}, u32[]{:S(2)}, u32[]{:S(2)}) collective-permute-start(bf16[2,120,512]{2,1,0:T(8,128)(2,1)S(1)} %fusion.11.act_ref), channel_id=1, source_target_pairs={{1,0},{2,1},{3,2},{4,3},{5,4},{6,5},{7,6},{8,7},{9,8},{10,9},{11,1... | collective-permute-start | bytes 737288 | tf_op jit(solution)/shard_map/ppermute | solution.py:525
  5.1 3.1 %collective-permute-start = (bf16[2,120,512]{2,1,0:T(8,128)(2,1)S(1)}, bf16[2,120,512]{2,1,0:T(8,128)(2,1)S(1)}, u32[]{:S(2)}, u32[]{:S(2)}) collective-permute-start(bf16[2,120,512]{2,1,0:T(8,128)(2,1)S(1)} %fusion.11.act_ref), channel_id=1, source_target_pairs={{0,1},{1,2},{2,3},{3,4},{4,5},{5,6},{6,7},{7,8},{8,9},{9,10},{10,1... | collective-permute-start | bytes 737288 | tf_op jit(solution)/shard_map/ppermute | solution.py:525
  8.2 2.3 %copy-done = bf16[4608,512]{1,0:T(8,128)(2,1)S(1)} copy-done((bf16[4608,512]{1,0:T(8,128)(2,1)S(1)}, bf16[4608,512]{1,0:T(8,128)(2,1)}, u32[]{:S(2)}) %copy-start) | copy-done | bytes 4718616
  12.4 2.3 %add_multiply_fusion = (f32[2,120,512]{2,1,0:T(8,128)}, bf16[2,120,512]{2,1,0:T(8,128)(2,1)S(1)}) fusion(bf16[2,120,4608]{2,1,0:T(8,128)(2,1)S(1)} %fusion.17, bf16[4608,512]{1,0:T(8,128)(2,1)S(1)} %shard_map.85), kind=kOutput, calls=%fused_computation.25 | convolution fusion | flops 1133568000 | bytes 7667712 | tf_op jit(solution)/shard_map/dot_general | solution.py:519
  14.7 3.5 %collective-permute-start.2 = (bf16[2,120,512]{2,1,0:T(8,128)(2,1)S(1)}, bf16[2,120,512]{2,1,0:T(8,128)(2,1)S(1)}, u32[]{:S(2)}, u32[]{:S(2)}) collective-permute-start(bf16[2,120,512]{2,1,0:T(8,128)(2,1)S(1)} %get-tuple-element.83), channel_id=1, source_target_pairs={{0,32},{32,64},{64,96},{1,33},{33,65},{65,97},{2,34},{34,66},{66,9... | collective-permute-start | bytes 737288 | tf_op jit(solution)/shard_map/ppermute | solution.py:525
  18.3 5.7 %collective-permute-done.2 = bf16[2,120,512]{2,1,0:T(8,128)(2,1)S(1)} collective-permute-done((bf16[2,120,512]{2,1,0:T(8,128)(2,1)S(1)}, bf16[2,120,512]{2,1,0:T(8,128)(2,1)S(1)}, u32[]{:S(2)}, u32[]{:S(2)}) %collective-permute-start.2) | collective-permute-done | bytes 245792 | tf_op jit(solution)/shard_map/ppermute | solution.py:525
  24.0 2.8 %shard_map.86 = (f32[2,120,512]{2,1,0:T(8,128)S(1)}, bf16[2,120,512]{2,1,0:T(8,128)(2,1)S(1)}, bf16[2,16,120,128]{3,2,1,0:T(8,128)(2,1)}) custom-call(bf16[2,120,512]{2,1,0:T(8,128)(2,1)S(1)} %bitcast.68, bf16[4,120,512]{2,1,0:T(8,128)(2,1)S(1)} %pad_maximum_fusion.bext_ref.refs_2_, bf16[2,120,512]{2,1,0:T(8,128)(2,1)S(1)} %bitcast.73, ...), custom_call_target="tpu_custom_call" | custom-call | flops 2000000000 | bytes 6291456 | tf_op jit(solution)/shard_map/pallas_call | solution.py:42
  27.6 8.8 %all-to-all-start = ((bf16[32,120,128]{2,1,0:T(8,128)(2,1)}), bf16[32,120,128]{2,1,0:T(8,128)(2,1)S(1)}, u32[]{:S(2)}, u32[]{:S(2)}) async-start(bf16[32,120,128]{2,1,0:T(8,128)(2,1)} %bitcast.17), calls=%async_computation | async-start | bytes 1966080 | tf_op jit(solution)/shard_map/all_to_all | solution.py:584
  44.1 8.7 %all-to-all-done = bf16[32,120,128]{2,1,0:T(8,128)(2,1)S(1)} async-done(((bf16[32,120,128]{2,1,0:T(8,128)(2,1)}), bf16[32,120,128]{2,1,0:T(8,128)(2,1)S(1)}, u32[]{:S(2)}, u32[]{:S(2)}) %all-to-all-start) | async-done | bytes 983072 | tf_op jit(solution)/shard_map/all_to_all | solution.py:584
  52.8 3.9 %all-to-all-start.1 = ((bf16[8,4,120,256]{3,2,1,0:T(8,128)(2,1)}), bf16[8,4,120,256]{3,2,1,0:T(8,128)(2,1)S(1)}, u32[]{:S(2)}, u32[]{:S(2)}) async-start(bf16[8,4,120,256]{3,2,1,0:T(8,128)(2,1)} %shard_map.87), calls=%async_computation.1 | async-start | bytes 3932160 | tf_op jit(solution)/shard_map/all_to_all | solution.py:540
  56.7 47.2 %shard_map.88 = bf16[3840,128]{1,0:T(8,128)(2,1)S(1)} custom-call(bf16[3840,128]{1,0:T(8,128)(2,1)S(1)} %bitcast.70), custom_call_target="tpu_custom_call" | custom-call | flops 22649241600 | bytes 1966080 | tf_op jit(solution)/shard_map/pallas_call | solution.py:190
  104.9 5.2 %all-to-all-start.2 = ((bf16[32,120,128]{2,1,0:T(8,128)(2,1)}), bf16[32,120,128]{2,1,0:T(8,128)(2,1)S(1)}, u32[]{:S(2)}, u32[]{:S(2)}) async-start(bf16[32,120,128]{2,1,0:T(8,128)(2,1)} %bitcast.72), calls=%async_computation.2 | async-start | bytes 1966080 | tf_op jit(solution)/shard_map/all_to_all | solution.py:594
  115.5 11.0 %all-to-all-done.2 = bf16[32,120,128]{2,1,0:T(8,128)(2,1)S(1)} async-done(((bf16[32,120,128]{2,1,0:T(8,128)(2,1)}), bf16[32,120,128]{2,1,0:T(8,128)(2,1)S(1)}, u32[]{:S(2)}, u32[]{:S(2)}) %all-to-all-start.2) | async-done | bytes 983072 | tf_op jit(solution)/shard_map/all_to_all | solution.py:594
  142.6 2.0 shard_map.93
  145.3 5.0 %all-to-all-start.3 = ((bf16[8,2,120,128]{3,2,1,0:T(8,128)(2,1)}), bf16[8,2,120,128]{3,2,1,0:T(8,128)(2,1)}, u32[]{:S(2)}, u32[]{:S(2)}) async-start(bf16[8,2,120,128]{3,2,1,0:T(8,128)(2,1)} %get-tuple-element.66), calls=%async_computation.3 | async-start | bytes 983040 | tf_op jit(solution)/shard_map/all_to_all | solution.py:540
  150.3 2.0 %collective-permute-start.13 = (bf16[2,120,512]{2,1,0:T(8,128)(2,1)}, bf16[2,120,512]{2,1,0:T(8,128)(2,1)S(1)}, u32[]{:S(2)}, u32[]{:S(2)}) collective-permute-start(bf16[2,120,512]{2,1,0:T(8,128)(2,1)} %copy-done.22), channel_id=1, source_target_pairs={{1,0},{2,1},{3,2},{4,3},{5,4},{6,5},{7,6},{8,7},{9,8},{10,9},{11,1... | collective-permute-start | bytes 737288 | tf_op jit(solution)/shard_map/ppermute | solution.py:525
  152.4 3.5 %collective-permute-start.12 = (bf16[2,120,512]{2,1,0:T(8,128)(2,1)}, bf16[2,120,512]{2,1,0:T(8,128)(2,1)S(1)}, u32[]{:S(2)}, u32[]{:S(2)}) collective-permute-start(bf16[2,120,512]{2,1,0:T(8,128)(2,1)} %copy-done.22), channel_id=1, source_target_pairs={{0,1},{1,2},{2,3},{3,4},{4,5},{5,6},{6,7},{7,8},{8,9},{9,10},{10,1... | collective-permute-start | bytes 737288 | tf_op jit(solution)/shard_map/ppermute | solution.py:525
  156.9 2.7 %all-to-all-done.3.dpre_ref = bf16[8,2,120,128]{3,2,1,0:T(8,128)(2,1)} async-done(((bf16[8,2,120,128]{3,2,1,0:T(8,128)(2,1)}), bf16[8,2,120,128]{3,2,1,0:T(8,128)(2,1)}, u32[]{:S(2)}, u32[]{:S(2)}) %all-to-all-start.3) | async-done | bytes 491552 | tf_op jit(solution)/shard_map/all_to_all | solution.py:540
  159.6 2.8 %collective-permute-done.9.refs_1_ = bf16[56,16,256]{2,1,0:T(8,128)(2,1)} collective-permute-done((bf16[56,16,256]{2,1,0:T(8,128)(2,1)S(1)}, bf16[56,16,256]{2,1,0:T(8,128)(2,1)}, u32[]{:S(2)}, u32[]{:S(2)}) %collective-permute-start.9) | collective-permute-done | bytes 458784 | tf_op jit(solution)/shard_map/ppermute | solution.py:545
  162.7 5.8 %shard_map.94 = bf16[128,32,128]{2,1,0:T(8,128)(2,1)} custom-call(bf16[3,2,256,1280]{3,2,1,0:T(8,128)(2,1)} %copy-done.2, bf16[8,2,120,128]{3,2,1,0:T(8,128)(2,1)} %all-to-all-done.3.dpre_ref, bf16[56,16,256]{2,1,0:T(8,128)(2,1)} %copy-done.28, bf16[56,16,256]{2,1,0:T(8,128)(2,1)} %collective-permute-done.9.refs_1_, ...), custom_call_target="tpu_custom_call" | custom-call | flops 2000000000 | bytes 10485760 | tf_op jit(solution)/shard_map/pallas_call | solution.py:397
  168.5 11.4 %all-to-all-start.4 = ((bf16[128,32,128]{2,1,0:T(8,128)(2,1)}), bf16[128,32,128]{2,1,0:T(8,128)(2,1)S(1)}, u32[]{:S(2)}, u32[]{:S(2)}) async-start(bf16[128,32,128]{2,1,0:T(8,128)(2,1)} %shard_map.94), calls=%async_computation.4 | async-start | bytes 2097152 | tf_op jit(solution)/shard_map/all_to_all | solution.py:615
  180.0 2.3 %copy-done.1 = bf16[4608,512]{1,0:T(8,128)(2,1)S(1)} copy-done((bf16[4608,512]{1,0:T(8,128)(2,1)S(1)}, bf16[4608,512]{1,0:T(8,128)(2,1)}, u32[]{:S(2)}) %copy-start.1) | copy-done | bytes 4718616
  182.3 3.9 %shard_map.95 = bf16[2,120,512]{2,1,0:T(8,128)(2,1)} custom-call(bf16[2,120,512]{2,1,0:T(8,128)(2,1)S(1)} %copy-done.23, bf16[2,120,512]{2,1,0:T(8,128)(2,1)S(1)} %collective-permute-done.12.above_ref, bf16[2,120,512]{2,1,0:T(8,128)(2,1)S(1)} %collective-permute-done.13.below_ref, f32[2,120,512]{2,1,0:T(8,128)S(1)} %copy-done.30, ...), custom_call_target="tpu_custom_call" | custom-call | flops 2000000000 | bytes 8388608 | tf_op jit(solution)/shard_map/pallas_call | solution.py:505
  186.2 13.1 %all-to-all-done.4.terms_ref = bf16[128,32,128]{2,1,0:T(8,128)(2,1)S(1)} async-done(((bf16[128,32,128]{2,1,0:T(8,128)(2,1)}), bf16[128,32,128]{2,1,0:T(8,128)(2,1)S(1)}, u32[]{:S(2)}, u32[]{:S(2)}) %all-to-all-start.4) | async-done | bytes 1048608 | tf_op jit(solution)/shard_map/all_to_all | solution.py:615
  (119 shorter events, 36.6 us)
Async XLA Ops:
  1.7 9.9 %collective-permute-start.1 = (bf16[2,120,512]{2,1,0:T(8,128)(2,1)S(1)}, bf16[2,120,512]{2,1,0:T(8,128)(2,1)S(1)}, u32[]{:S(2)}, u32[]{:S(2)}) collective-permute-start(bf16[2,120,512]{2,1,0:T(8,128)(2,1)S(1)} %fusion.11.act_ref), channel_id=1, source_target_pairs={{1,0},{2,1},{3,2},{4,3},{5,4},{6,5},{7,6},{8,7},{9,8},{10,9},{11,1... | collective-permute-start | bytes 737288 | tf_op jit(solution)/shard_map/ppermute | solution.py:525
  5.1 6.6 %collective-permute-start = (bf16[2,120,512]{2,1,0:T(8,128)(2,1)S(1)}, bf16[2,120,512]{2,1,0:T(8,128)(2,1)S(1)}, u32[]{:S(2)}, u32[]{:S(2)}) collective-permute-start(bf16[2,120,512]{2,1,0:T(8,128)(2,1)S(1)} %fusion.11.act_ref), channel_id=1, source_target_pairs={{0,1},{1,2},{2,3},{3,4},{4,5},{5,6},{6,7},{7,8},{8,9},{9,10},{10,1... | collective-permute-start | bytes 737288 | tf_op jit(solution)/shard_map/ppermute | solution.py:525
  14.7 9.2 %collective-permute-start.2 = (bf16[2,120,512]{2,1,0:T(8,128)(2,1)S(1)}, bf16[2,120,512]{2,1,0:T(8,128)(2,1)S(1)}, u32[]{:S(2)}, u32[]{:S(2)}) collective-permute-start(bf16[2,120,512]{2,1,0:T(8,128)(2,1)S(1)} %get-tuple-element.83), channel_id=1, source_target_pairs={{0,32},{32,64},{64,96},{1,33},{33,65},{65,97},{2,34},{34,66},{66,9... | collective-permute-start | bytes 737288 | tf_op jit(solution)/shard_map/ppermute | solution.py:525
  27.6 25.2 %all-to-all-start = ((bf16[32,120,128]{2,1,0:T(8,128)(2,1)}), bf16[32,120,128]{2,1,0:T(8,128)(2,1)S(1)}, u32[]{:S(2)}, u32[]{:S(2)}) async-start(bf16[32,120,128]{2,1,0:T(8,128)(2,1)} %bitcast.17), calls=%async_computation | async-start | bytes 1966080 | tf_op jit(solution)/shard_map/all_to_all | solution.py:584
  36.4 7.0 %collective-permute-start.5 = (bf16[4,120,512]{2,1,0:T(8,128)(2,1)S(1)}, bf16[4,120,512]{2,1,0:T(8,128)(2,1)S(1)}, u32[]{:S(2)}, u32[]{:S(2)}) collective-permute-start(bf16[4,120,512]{2,1,0:T(8,128)(2,1)S(1)} %pad_maximum_fusion.bext_ref.refs_2_), channel_id=1, source_target_pairs={{0,1},{1,0},{2,3},{3,2},{4,5},{5,4},{6,7},{7,6},{8,9},{9,8},{10,11... | collective-permute-start | bytes 1474568 | tf_op jit(solution)/shard_map/ppermute | solution.py:530
  37.4 5.2 %collective-permute-start.4 = (bf16[2,120,512]{2,1,0:T(8,128)(2,1)S(1)}, bf16[2,120,512]{2,1,0:T(8,128)(2,1)S(1)}, u32[]{:S(2)}, u32[]{:S(2)}) collective-permute-start(bf16[2,120,512]{2,1,0:T(8,128)(2,1)S(1)} %get-tuple-element.42.refs_0_), channel_id=1, source_target_pairs={{0,1},{1,0},{2,3},{3,2},{4,5},{5,4},{6,7},{7,6},{8,9},{9,8},{10,11... | collective-permute-start | bytes 737288 | tf_op jit(solution)/shard_map/ppermute | solution.py:530
  39.3 2.7 %collective-permute-start.3 = (bf16[2,120,256]{2,1,0:T(8,128)(2,1)S(1)}, bf16[2,120,256]{2,1,0:T(8,128)(2,1)S(1)}, u32[]{:S(2)}, u32[]{:S(2)}) collective-permute-start(bf16[2,120,256]{2,1,0:T(8,128)(2,1)S(1)} %bitcast.80), channel_id=1, source_target_pairs={{0,1},{1,0},{2,3},{3,2},{4,5},{5,4},{6,7},{7,6},{8,9},{9,8},{10,11... | collective-permute-start | bytes 368648 | tf_op jit(solution)/shard_map/ppermute | solution.py:530
  52.8 52.1 %all-to-all-start.1 = ((bf16[8,4,120,256]{3,2,1,0:T(8,128)(2,1)}), bf16[8,4,120,256]{3,2,1,0:T(8,128)(2,1)S(1)}, u32[]{:S(2)}, u32[]{:S(2)}) async-start(bf16[8,4,120,256]{3,2,1,0:T(8,128)(2,1)} %shard_map.87), calls=%async_computation.1 | async-start | bytes 3932160 | tf_op jit(solution)/shard_map/all_to_all | solution.py:540
  104.9 21.7 %all-to-all-start.2 = ((bf16[32,120,128]{2,1,0:T(8,128)(2,1)}), bf16[32,120,128]{2,1,0:T(8,128)(2,1)S(1)}, u32[]{:S(2)}, u32[]{:S(2)}) async-start(bf16[32,120,128]{2,1,0:T(8,128)(2,1)} %bitcast.72), calls=%async_computation.2 | async-start | bytes 1966080 | tf_op jit(solution)/shard_map/all_to_all | solution.py:594
  115.5 17.8 %copy-start.15 = (bf16[2,120,1,256]{3,1,0,2:T(8,128)(2,1)S(1)}, bf16[2,120,1,256]{3,1,0,2:T(8,128)(2,1)}, u32[]{:S(2)}) copy-start(bf16[2,120,1,256]{3,1,0,2:T(8,128)(2,1)} %copy.19) | copy-start | bytes 368644
  131.1 2.2 %collective-permute-start.8 = (bf16[2,120,1024]{2,1,0:T(8,128)(2,1)S(1)}, bf16[2,120,1024]{2,1,0:T(8,128)(2,1)S(1)}, u32[]{:S(2)}, u32[]{:S(2)}) collective-permute-start(bf16[2,120,1024]{2,1,0:T(8,128)(2,1)S(1)} %get-tuple-element.61), channel_id=1, source_target_pairs={{0,1},{1,0},{2,3},{3,2},{4,5},{5,4},{6,7},{7,6},{8,9},{9,8},{10,11... | collective-permute-start | bytes 1474568 | tf_op jit(solution)/shard_map/ppermute | solution.py:530
  131.5 1.8 collective-permute-start.7
  131.6 11.0 %collective-permute-start.6 = (bf16[2,120,512]{2,1,0:T(8,128)(2,1)S(1)}, bf16[2,120,512]{2,1,0:T(8,128)(2,1)S(1)}, u32[]{:S(2)}, u32[]{:S(2)}) collective-permute-start(bf16[2,120,512]{2,1,0:T(8,128)(2,1)S(1)} %get-tuple-element.56.own_ref), channel_id=1, source_target_pairs={{32,0},{64,32},{96,64},{33,1},{65,33},{97,65},{34,2},{66,34},{98,6... | collective-permute-start | bytes 737288 | tf_op jit(solution)/shard_map/ppermute | solution.py:525
  139.4 16.5 %copy-start.8 = (bf16[512,512]{1,0:T(8,128)(2,1)S(1)}, bf16[512,512]{1,0:T(8,128)(2,1)}, u32[]{:S(2)}) copy-start(bf16[512,512]{1,0:T(8,128)(2,1)} %ow_ref.1) | copy-start | bytes 1572868
  139.4 16.5 %copy-start.11 = (f32[2,120,512]{2,1,0:T(8,128)S(1)}, f32[2,120,512]{2,1,0:T(8,128)}, u32[]{:S(2)}) copy-start(f32[2,120,512]{2,1,0:T(8,128)} %copy-done.10) | copy-start | bytes 1474564
  139.4 22.9 %collective-permute-start.9 = (bf16[56,16,256]{2,1,0:T(8,128)(2,1)S(1)}, bf16[56,16,256]{2,1,0:T(8,128)(2,1)}, u32[]{:S(2)}, u32[]{:S(2)}) collective-permute-start(bf16[56,16,256]{2,1,0:T(8,128)(2,1)S(1)} %get-tuple-element.70), channel_id=1, source_target_pairs={{0,8},{1,9},{2,10},{3,11},{4,12},{5,13},{6,14},{7,15},{8,16},{9,17... | collective-permute-start | bytes 1376264 | tf_op jit(solution)/shard_map/ppermute | solution.py:545
  139.5 22.9 %collective-permute-start.10 = (bf16[56,16,256]{2,1,0:T(8,128)(2,1)S(1)}, bf16[56,16,256]{2,1,0:T(8,128)(2,1)}, u32[]{:S(2)}, u32[]{:S(2)}) collective-permute-start(bf16[56,16,256]{2,1,0:T(8,128)(2,1)S(1)} %get-tuple-element.71), channel_id=1, source_target_pairs={{0,16},{1,17},{2,18},{3,19},{4,20},{5,21},{6,22},{7,23},{8,24},{9,... | collective-permute-start | bytes 1376264 | tf_op jit(solution)/shard_map/ppermute | solution.py:545
  141.2 21.5 %collective-permute-start.11 = (bf16[56,16,256]{2,1,0:T(8,128)(2,1)S(1)}, bf16[56,16,256]{2,1,0:T(8,128)(2,1)}, u32[]{:S(2)}, u32[]{:S(2)}) collective-permute-start(bf16[56,16,256]{2,1,0:T(8,128)(2,1)S(1)} %get-tuple-element.72), channel_id=1, source_target_pairs={{0,24},{1,25},{2,26},{3,27},{4,28},{5,29},{6,30},{7,31},{8,0},{9,1... | collective-permute-start | bytes 1376264 | tf_op jit(solution)/shard_map/ppermute | solution.py:545
  145.3 14.3 %all-to-all-start.3 = ((bf16[8,2,120,128]{3,2,1,0:T(8,128)(2,1)}), bf16[8,2,120,128]{3,2,1,0:T(8,128)(2,1)}, u32[]{:S(2)}, u32[]{:S(2)}) async-start(bf16[8,2,120,128]{3,2,1,0:T(8,128)(2,1)} %get-tuple-element.66), calls=%async_computation.3 | async-start | bytes 983040 | tf_op jit(solution)/shard_map/all_to_all | solution.py:540
  150.3 18.2 %collective-permute-start.13 = (bf16[2,120,512]{2,1,0:T(8,128)(2,1)}, bf16[2,120,512]{2,1,0:T(8,128)(2,1)S(1)}, u32[]{:S(2)}, u32[]{:S(2)}) collective-permute-start(bf16[2,120,512]{2,1,0:T(8,128)(2,1)} %copy-done.22), channel_id=1, source_target_pairs={{1,0},{2,1},{3,2},{4,3},{5,4},{6,5},{7,6},{8,7},{9,8},{10,9},{11,1... | collective-permute-start | bytes 737288 | tf_op jit(solution)/shard_map/ppermute | solution.py:525
  152.4 16.1 %collective-permute-start.12 = (bf16[2,120,512]{2,1,0:T(8,128)(2,1)}, bf16[2,120,512]{2,1,0:T(8,128)(2,1)S(1)}, u32[]{:S(2)}, u32[]{:S(2)}) collective-permute-start(bf16[2,120,512]{2,1,0:T(8,128)(2,1)} %copy-done.22), channel_id=1, source_target_pairs={{0,1},{1,2},{2,3},{3,4},{4,5},{5,6},{6,7},{7,8},{8,9},{9,10},{10,1... | collective-permute-start | bytes 737288 | tf_op jit(solution)/shard_map/ppermute | solution.py:525
  159.6 20.4 %copy-start.23 = (bf16[2,120,512]{2,1,0:T(8,128)(2,1)S(1)}, bf16[2,120,512]{2,1,0:T(8,128)(2,1)}, u32[]{:S(2)}) copy-start(bf16[2,120,512]{2,1,0:T(8,128)(2,1)} %copy-done.22) | copy-start | bytes 737284
  162.4 17.5 %copy-start.30 = (f32[2,120,512]{2,1,0:T(8,128)S(1)}, f32[2,120,512]{2,1,0:T(8,128)}, u32[]{:S(2)}) copy-start(f32[2,120,512]{2,1,0:T(8,128)} %copy-done.29) | copy-start | bytes 1474564
  168.5 30.8 %all-to-all-start.4 = ((bf16[128,32,128]{2,1,0:T(8,128)(2,1)}), bf16[128,32,128]{2,1,0:T(8,128)(2,1)S(1)}, u32[]{:S(2)}, u32[]{:S(2)}) async-start(bf16[128,32,128]{2,1,0:T(8,128)(2,1)} %shard_map.94), calls=%async_computation.4 | async-start | bytes 2097152 | tf_op jit(solution)/shard_map/all_to_all | solution.py:615
  (32 other events, 122.0 us)
where the time goes:
time: 201 us; the launch traced here: 200 us
  Pallas kernels  69.4 us (35%)
  starting transfers between devices  55.7 us (28%)
  waiting for transfers between devices  44.8 us (22%)
  local copies, waits for them, and re-layouts  24.1 us (12%)
  matrix products  3.24 us (2%)
    pallas_call x1, Pallas kernels, attn(): pl.pallas_call(functools.partial(attn_kernel, 1.0 / math.sqrt(32), tq, ck...  47.2 us
    unnamed x82, local copies, waits for them, and re-layouts  21.8 us
    ppermute x6, starting transfers between devices, shift(): return lax.ppermute(x, axis, pairs)  16.8 us
    all_to_all x1, waiting for transfers between devices, per_device(): terms = lax.all_to_all(terms, ('tm', 'space'), 0, 0, tiled=True)  13.1 us
    all_to_all x1, starting transfers between devices, per_device(): terms = lax.all_to_all(terms, ('tm', 'space'), 0, 0, tiled=True)  11.4 us
    all_to_all x1, waiting for transfers between devices, per_device(): outs = lax.all_to_all(outs, 'space', 0, 0, tiled=True)  11 us
    all_to_all x2, starting transfers between devices, exchange(): lax.all_to_all(x, 'space', 0, 0, axis_index_groups=groups, tiled=True)  8.91 us
    all_to_all x1, starting transfers between devices, per_device(): items = lax.all_to_all(items, 'space', 0, 0, tiled=True)  8.76 us
  transfers between devices with their start and end apart: 19, of which 8 were waited for; matrix products, arithmetic and copies ran while one was open for 2% of the time, Pallas kernels for 32%

commit v1 on v0

--- a/solution.py
+++ b/solution.py
@@ -42,7 +42,7 @@
     return pl.pallas_call(
         proj_kernel,
         out_shape=(
-            jax.ShapeDtypeStruct((frames, width, chans), F32),
+            pltpu.HBM((frames, width, chans), F32),
             jax.ShapeDtypeStruct((frames, width, chans), BF),
             jax.ShapeDtypeStruct((frames, HEADS, width, 4 * chans // HEADS), BF),
         ),
@@ -51,22 +51,31 @@
     )(x, bext, cot, tw, qw, ow)
 
 
-def post_kernel(core_ref, z_ref, cot_ref, qw_ref, attn_ref, dres_ref, dresb_ref, mine_ref, other_ref):
+def post_kernel(
+    core_ref, z_ref, cot_ref, qw_hbm, attn_ref, dres_hbm, dresb_ref, mine_hbm, other_ref, qw_ref, dres_ref, mine_ref, sems
+):
     frames, width, chans = cot_ref.shape
     d = chans // HEADS
     half = chans // 2
+    weight = pltpu.make_async_copy(qw_hbm, qw_ref, sems.at[0])
+    weight.start()
     all_parts = []
     for f in range(frames):
         heads = [z_ref[f, h].astype(F32) for h in range(HEADS)]
-        dres = cot_ref[f].astype(F32)
         parts = [jnp.concatenate([z[:, p * d : (p + 1) * d] for z in heads], axis=1).astype(BF) for p in range(4)]
         attn_ref[f] = parts[0]
+        all_parts.append(parts[1:])
+    weight.wait()
+    for f in range(frames):
+        dres = cot_ref[f].astype(F32)
         for p in range(3):
-            dres = dres + dot_nt(parts[p + 1], qw_ref[:, p * chans : (p + 1) * chans])
+            dres = dres + dot_nt(all_parts[f][p], qw_ref[:, p * chans : (p + 1) * chans])
         dres_ref[f] = dres
         dresb = dres.astype(BF)
         dresb_ref[f] = dresb
-        all_parts.append(parts[1:] + [dresb])
+        all_parts[f].append(dresb)
+    sent = pltpu.make_async_copy(dres_ref, dres_hbm, sems.at[1])
+    sent.start()
 
     def store(first, second):
         for f in range(frames):
@@ -82,22 +91,35 @@
     def _():
         store(other_ref, mine_ref)
 
+    kept = pltpu.make_async_copy(mine_ref, mine_hbm, sems.at[2])
+    kept.start()
+    sent.wait()
+    kept.wait()
+
 
 def post(core, z, cot, qw):
     frames, width, chans = cot.shape
+    vmem, hbm = pl.BlockSpec(memory_space=pltpu.VMEM), pl.BlockSpec(memory_space=pltpu.HBM)
     return pl.pallas_call(
         post_kernel,
         out_shape=(
             jax.ShapeDtypeStruct((frames, width, chans), BF),
-            jax.ShapeDtypeStruct((frames, width, chans), F32),
+            pltpu.HBM((frames, width, chans), F32),
             jax.ShapeDtypeStruct((frames, width, chans), BF),
-            jax.ShapeDtypeStruct((frames, width, 2 * chans), BF),
+            pltpu.HBM((frames, width, 2 * chans), BF),
             jax.ShapeDtypeStruct((frames, width, 2 * chans), BF),
         ),
-        in_specs=[pl.BlockSpec(memory_space=pltpu.SMEM)] + [pl.BlockSpec(memory_space=pltpu.VMEM)] * 3,
+        in_specs=[pl.BlockSpec(memory_space=pltpu.SMEM), vmem, vmem, hbm],
+        out_specs=(vmem, hbm, vmem, hbm, vmem),
+        scratch_shapes=[
+            pltpu.VMEM(qw.shape, BF),
+            pltpu.VMEM((frames, width, chans), F32),
+            pltpu.VMEM((frames, width, 2 * chans), BF),
+            pltpu.SemaphoreType.DMA((3,)),
+        ],
         compiler_params=pltpu.CompilerParams(vmem_limit_bytes=32 << 20),
         cost_estimate=pl.CostEstimate(flops=10**9, bytes_accessed=6 << 20, transcendentals=0),
-    )(core, z, cot, qw)
+    )(core, z, cot, pltpu.with_memory_space_constraint(qw, pltpu.HBM))
 
 
 def fetch_kernel(w_ref, out_ref):
@@ -192,7 +214,7 @@
         grid=(tok // tq,),
         in_specs=[pl.BlockSpec((tok, 128), lambda i: (0, 0))],
         out_specs=pl.BlockSpec((tok, 128), lambda i: (0, 0)),
-        out_shape=jax.ShapeDtypeStruct((tok, 128), BF),
+        out_shape=pltpu.HBM((tok, 128), BF),
         scratch_shapes=[pltpu.VMEM((tok, 128), BF), pltpu.VMEM((32, tok), BF), pltpu.VMEM((48, tok), BF),
                         pltpu.VMEM((tok, tq), F32), pltpu.VMEM((tok, tq), BF), pltpu.VMEM((tok, 128), F32)],
         compiler_params=pltpu.CompilerParams(vmem_limit_bytes=48 << 20),
@@ -258,7 +280,7 @@
     group, _, _, chans = r.shape
     return pl.pallas_call(
         turn_kernel,
-        out_shape=jax.ShapeDtypeStruct((3, frames, chans, (group + 2) * LANES), BF),
+        out_shape=pltpu.HBM((3, frames, chans, (group + 2) * LANES), BF),
         compiler_params=CALL(),
         cost_estimate=cost(1e9, 6 << 20),
     )(r)
@@ -279,17 +301,22 @@
     return pl.pallas_call(
         turn_pair_kernel,
         out_shape=tuple(
-            jax.ShapeDtypeStruct((chans, 2 * x.shape[0] * LANES), BF) for x in (own_r, own_b)
+            pltpu.HBM((chans, 2 * x.shape[0] * LANES), BF) for x in (own_r, own_b)
         ),
         compiler_params=CALL(),
         cost_estimate=cost(1e9, 4 << 20),
     )(own_r, other_r, own_b, other_b)
 
 
-def local_terms_kernel(
-    line_ref, rt_ref, bt_ref, a0_ref, a1_ref, p0_ref, p1_ref, c0_ref, c1_ref, *refs
-):
-    outs, (at_ref, pay_ref, cot_ref, mix_ref, out_ref) = refs[:4], refs[4:]
+def local_terms_kernel(line_ref, a0_ref, a1_ref, p1_ref, *refs):
+    far, outs, scratch = refs[:5], refs[5:9], refs[9:]
+    near, (at_ref, pay_ref, cot_ref, mix_ref, out_ref, sems) = scratch[:5], scratch[5:]
+    rt_ref, bt_ref, p0_ref, c0_ref, c1_ref = near
+    copies = [pltpu.make_async_copy(src, dst, sems.at[k]) for k, (src, dst) in enumerate(zip(far, near))]
+    for copy in copies:
+        copy.start()
+    for copy in copies:
+        copy.wait()
     frames, width, chans = a0_ref.shape
     half = chans // 2
     for d, (a, p, c) in enumerate(((a0_ref, p0_ref, c0_ref), (a1_ref, p1_ref, c1_ref))):
@@ -331,20 +358,25 @@
     half = chans // 2
     span = 2 * frames * LANES
     piece = (7 * chans // 64, 16, half)
+    far = (rt, bt, pay[0], cot[0], cot[1])
     return pl.pallas_call(
         local_terms_kernel,
-        out_shape=(jax.ShapeDtypeStruct(piece, BF),) * 4,
-        in_specs=[pl.BlockSpec(memory_space=pltpu.SMEM)] + [pl.BlockSpec(memory_space=pltpu.VMEM)] * 8,
-        scratch_shapes=[
+        out_shape=(pltpu.HBM(piece, BF),) + (jax.ShapeDtypeStruct(piece, BF),) * 3,
+        in_specs=[pl.BlockSpec(memory_space=pltpu.SMEM)]
+        + [pl.BlockSpec(memory_space=pltpu.VMEM)] * 3
+        + [pl.BlockSpec(memory_space=pltpu.HBM)] * 5,
+        scratch_shapes=[pltpu.VMEM(x.shape, BF) for x in far]
+        + [
             pltpu.VMEM((chans, span), BF),
             pltpu.VMEM((span, 4 * half), BF),
             pltpu.VMEM((span, half), BF),
             pltpu.VMEM((half // LANES, 3 * chans, LANES), F32),
             pltpu.VMEM((4,) + piece, BF),
+            pltpu.SemaphoreType.DMA((5,)),
         ],
         compiler_params=CALL(),
         cost_estimate=cost(2e9, 10 << 20),
-    )(line, rt, bt, *atted, *pay, *cot)
+    )(line, *atted, pay[1], *[pltpu.with_memory_space_constraint(v, pltpu.HBM) for v in far])
 
 
 def conv_terms_kernel(at_ref, dpre_ref, *refs):
@@ -474,7 +506,7 @@
     return pl.pallas_call(
         dpre_kernel,
         out_shape=(
-            jax.ShapeDtypeStruct((frames, width, chans), BF),
+            pltpu.HBM((frames, width, chans), BF),
             jax.ShapeDtypeStruct((GROUP, frames, width, 2 * chans // GROUP), BF),
         ),
         compiler_params=CALL(),

time: 201 us -> 199 us (0.990)
  local copies, waits for them, and re-layouts: 24.1 us -> 11.8 us
  Pallas kernels: 69.4 us -> 79.1 us
    unnamed x82 -> x52, local copies, waits for them, and re-layouts: 21.8 us -> 9.4 us
    pallas_call x5, Pallas kernels: 8.25 us -> 14.2 us  [the longest x1 4.56 us: local_terms(): pl.pallas_call(local_terms_kernel, out_shape=(pltpu.HBM(piece, BF),) + (j...]
    pallas_call x1, Pallas kernels: 1.48 us -> 4.34 us  [post(): pl.pallas_call(post_kernel, out_shape=(jax.ShapeDtypeStruct((frames, widt...]
  transfers between devices with their start and end apart: 19 -> 19, of which waited for: 8 -> 9; matrix products, arithmetic and copies ran while one was open for 2% -> 3% of each run, Pallas kernels for 32% -> 36%
where the time goes in v1:
time: 199 us; the launch traced here: 198 us
  Pallas kernels  79.1 us (40%)
  starting transfers between devices  55 us (28%)
  waiting for transfers between devices  44.8 us (23%)
  local copies, waits for them, and re-layouts  11.8 us (6%)
  matrix products  4.31 us (2%)
    pallas_call x1, Pallas kernels, attn(): pl.pallas_call(functools.partial(attn_kernel, 1.0 / math.sqrt(32), tq, ck...  48.2 us
    ppermute x6, starting transfers between devices, shift(): return lax.ppermute(x, axis, pairs)  16.8 us
    all_to_all x1, waiting for transfers between devices, per_device(): terms = lax.all_to_all(terms, ('tm', 'space'), 0, 0, tiled=True)  12.1 us
    all_to_all x1, waiting for transfers between devices, per_device(): outs = lax.all_to_all(outs, 'space', 0, 0, tiled=True)  11.7 us
    all_to_all x1, starting transfers between devices, per_device(): terms = lax.all_to_all(terms, ('tm', 'space'), 0, 0, tiled=True)  11.4 us
    unnamed x52, local copies, waits for them, and re-layouts  9.4 us
    all_to_all x1, starting transfers between devices, per_device(): items = lax.all_to_all(items, 'space', 0, 0, tiled=True)  8.7 us
    all_to_all x1, waiting for transfers between devices, per_device(): items = lax.all_to_all(items, 'space', 0, 0, tiled=True)  8.7 us
  transfers between devices with their start and end apart: 19, of which 9 were waited for; matrix products, arithmetic and copies ran while one was open for 3% of the time, Pallas kernels for 36%

profile of v1, /device:TPU:1, one launch (start us, length us, event | category | flops | bytes accessed | tf_op | source)
XLA Modules:
  0.0 197.8 jit_solution(16602130837388724287)
XLA Ops:
  1.7 3.3 %collective-permute-start.1 = (bf16[2,120,512]{2,1,0:T(8,128)(2,1)S(1)}, bf16[2,120,512]{2,1,0:T(8,128)(2,1)S(1)}, u32[]{:S(2)}, u32[]{:S(2)}) collective-permute-start(bf16[2,120,512]{2,1,0:T(8,128)(2,1)S(1)} %fusion.11.act_ref), channel_id=1, source_target_pairs={{1,0},{2,1},{3,2},{4,3},{5,4},{6,5},{7,6},{8,7},{9,8},{10,9},{11,1... | collective-permute-start | bytes 737288 | tf_op jit(solution)/shard_map/ppermute | solution.py:557
  5.1 3.1 %collective-permute-start = (bf16[2,120,512]{2,1,0:T(8,128)(2,1)S(1)}, bf16[2,120,512]{2,1,0:T(8,128)(2,1)S(1)}, u32[]{:S(2)}, u32[]{:S(2)}) collective-permute-start(bf16[2,120,512]{2,1,0:T(8,128)(2,1)S(1)} %fusion.11.act_ref), channel_id=1, source_target_pairs={{0,1},{1,2},{2,3},{3,4},{4,5},{5,6},{6,7},{7,8},{8,9},{9,10},{10,1... | collective-permute-start | bytes 737288 | tf_op jit(solution)/shard_map/ppermute | solution.py:557
  8.2 2.3 %copy-done = bf16[4608,512]{1,0:T(8,128)(2,1)S(1)} copy-done((bf16[4608,512]{1,0:T(8,128)(2,1)S(1)}, bf16[4608,512]{1,0:T(8,128)(2,1)}, u32[]{:S(2)}) %copy-start) | copy-done | bytes 4718616
  12.4 2.3 %add_multiply_fusion = (f32[2,120,512]{2,1,0:T(8,128)}, bf16[2,120,512]{2,1,0:T(8,128)(2,1)S(1)}) fusion(bf16[2,120,4608]{2,1,0:T(8,128)(2,1)S(1)} %fusion.17, bf16[4608,512]{1,0:T(8,128)(2,1)S(1)} %shard_map.85), kind=kOutput, calls=%fused_computation.25 | convolution fusion | flops 1133568000 | bytes 7667712 | tf_op jit(solution)/shard_map/dot_general | solution.py:551
  14.7 3.5 %collective-permute-start.2 = (bf16[2,120,512]{2,1,0:T(8,128)(2,1)S(1)}, bf16[2,120,512]{2,1,0:T(8,128)(2,1)S(1)}, u32[]{:S(2)}, u32[]{:S(2)}) collective-permute-start(bf16[2,120,512]{2,1,0:T(8,128)(2,1)S(1)} %get-tuple-element.83), channel_id=1, source_target_pairs={{0,32},{32,64},{64,96},{1,33},{33,65},{65,97},{2,34},{34,66},{66,9... | collective-permute-start | bytes 737288 | tf_op jit(solution)/shard_map/ppermute | solution.py:557
  18.3 5.7 %collective-permute-done.2 = bf16[2,120,512]{2,1,0:T(8,128)(2,1)S(1)} collective-permute-done((bf16[2,120,512]{2,1,0:T(8,128)(2,1)S(1)}, bf16[2,120,512]{2,1,0:T(8,128)(2,1)S(1)}, u32[]{:S(2)}, u32[]{:S(2)}) %collective-permute-start.2) | collective-permute-done | bytes 245792 | tf_op jit(solution)/shard_map/ppermute | solution.py:557
  24.1 2.9 %shard_map.86 = (f32[2,120,512]{2,1,0:T(8,128)}, bf16[2,120,512]{2,1,0:T(8,128)(2,1)S(1)}, bf16[2,16,120,128]{3,2,1,0:T(8,128)(2,1)}) custom-call(bf16[2,120,512]{2,1,0:T(8,128)(2,1)S(1)} %bitcast.68, bf16[4,120,512]{2,1,0:T(8,128)(2,1)S(1)} %pad_maximum_fusion.bext_ref.refs_2_, bf16[2,120,512]{2,1,0:T(8,128)(2,1)S(1)} %bitcast.72, ...), custom_call_target="tpu_custom_call" | custom-call | flops 2000000000 | bytes 6291456 | tf_op jit(solution)/shard_map/pallas_call | solution.py:42
  27.0 8.7 %all-to-all-start = ((bf16[32,120,128]{2,1,0:T(8,128)(2,1)}), bf16[32,120,128]{2,1,0:T(8,128)(2,1)S(1)}, u32[]{:S(2)}, u32[]{:S(2)}) async-start(bf16[32,120,128]{2,1,0:T(8,128)(2,1)} %bitcast.17), calls=%async_computation | async-start | bytes 1966080 | tf_op jit(solution)/shard_map/all_to_all | solution.py:616
  43.4 8.7 %all-to-all-done = bf16[32,120,128]{2,1,0:T(8,128)(2,1)S(1)} async-done(((bf16[32,120,128]{2,1,0:T(8,128)(2,1)}), bf16[32,120,128]{2,1,0:T(8,128)(2,1)S(1)}, u32[]{:S(2)}, u32[]{:S(2)}) %all-to-all-start) | async-done | bytes 983072 | tf_op jit(solution)/shard_map/all_to_all | solution.py:616
  52.1 3.9 %all-to-all-start.1 = ((bf16[8,4,120,256]{3,2,1,0:T(8,128)(2,1)}), bf16[8,4,120,256]{3,2,1,0:T(8,128)(2,1)S(1)}, u32[]{:S(2)}, u32[]{:S(2)}) async-start(bf16[8,4,120,256]{3,2,1,0:T(8,128)(2,1)} %shard_map.87), calls=%async_computation.1 | async-start | bytes 3932160 | tf_op jit(solution)/shard_map/all_to_all | solution.py:572
  56.0 48.2 %shard_map.88 = bf16[3840,128]{1,0:T(8,128)(2,1)} custom-call(bf16[3840,128]{1,0:T(8,128)(2,1)S(1)} %bitcast.70), custom_call_target="tpu_custom_call" | custom-call | flops 22649241600 | bytes 1966080 | tf_op jit(solution)/shard_map/pallas_call | solution.py:212
  104.2 5.2 %all-to-all-start.2 = ((bf16[32,120,128]{2,1,0:T(8,128)(2,1)}), bf16[32,120,128]{2,1,0:T(8,128)(2,1)S(1)}, u32[]{:S(2)}, u32[]{:S(2)}) async-start(bf16[32,120,128]{2,1,0:T(8,128)(2,1)} %bitcast.76), calls=%async_computation.2 | async-start | bytes 1966080 | tf_op jit(solution)/shard_map/all_to_all | solution.py:626
  109.5 3.1 %shard_map.89.at_ref = bf16[3,2,256,1280]{3,2,1,0:T(8,128)(2,1)} custom-call(bf16[8,4,120,256]{3,2,1,0:T(8,128)(2,1)S(1)} %all-to-all-done.1.r_ref), custom_call_target="tpu_custom_call" | custom-call | flops 1000000000 | bytes 6291456 | tf_op jit(solution)/shard_map/pallas_call | solution.py:281
  114.2 11.7 %all-to-all-done.2 = bf16[32,120,128]{2,1,0:T(8,128)(2,1)S(1)} async-done(((bf16[32,120,128]{2,1,0:T(8,128)(2,1)}), bf16[32,120,128]{2,1,0:T(8,128)(2,1)S(1)}, u32[]{:S(2)}, u32[]{:S(2)}) %all-to-all-start.2) | async-done | bytes 983072 | tf_op jit(solution)/shard_map/all_to_all | solution.py:626
  125.9 4.3 %shard_map.91 = (bf16[2,120,512]{2,1,0:T(8,128)(2,1)S(1)}, f32[2,120,512]{2,1,0:T(8,128)}, bf16[2,120,512]{2,1,0:T(8,128)(2,1)S(1)}, bf16[2,120,1024]{2,1,0:T(8,128)(2,1)}, bf16[2,120,1024]{2,1,0:T(8,128)(2,1)S(1)}) custom-call(s32[1]{0:T(128)} %bitcast.14.core_ref, bf16[2,16,120,128]{3,2,1,0:T(8,128)(2,1)S(1)} %bitcast.71, ...), custom_call_target="tpu_custom_call" | custom-call | flops 1000000000 | bytes 6291456 | tf_op jit(solution)/shard_map/pallas_call | solution.py:103
  132.6 4.6 %shard_map.92 = (bf16[56,16,256]{2,1,0:T(8,128)(2,1)}, bf16[56,16,256]{2,1,0:T(8,128)(2,1)}, bf16[56,16,256]{2,1,0:T(8,128)(2,1)S(1)}, bf16[56,16,256]{2,1,0:T(8,128)(2,1)S(1)}) custom-call(s32[1]{0:T(128)} %bitcast.23.line_ref, bf16[2,120,512]{2,1,0:T(8,128)(2,1)S(1)} %get-tuple-element.55.a0_ref, bf16[2,120,512]{2,1,0:T(8,128)(2,1)S(1)} %collective-permute-done.7.a1_ref, ...), custom_call_target="tpu_custom_call" | custom-call | flops 2000000000 | bytes 10485760 | tf_op jit(solution)/shard_map/pallas_call | solution.py:362
  142.9 4.3 %all-to-all-start.3 = ((bf16[8,2,120,128]{3,2,1,0:T(8,128)(2,1)}), bf16[8,2,120,128]{3,2,1,0:T(8,128)(2,1)S(1)}, u32[]{:S(2)}, u32[]{:S(2)}) async-start(bf16[8,2,120,128]{3,2,1,0:T(8,128)(2,1)} %get-tuple-element.66), calls=%async_computation.3 | async-start | bytes 983040 | tf_op jit(solution)/shard_map/all_to_all | solution.py:572
  149.2 3.5 %collective-permute-start.12 = (bf16[2,120,512]{2,1,0:T(8,128)(2,1)}, bf16[2,120,512]{2,1,0:T(8,128)(2,1)S(1)}, u32[]{:S(2)}, u32[]{:S(2)}) collective-permute-start(bf16[2,120,512]{2,1,0:T(8,128)(2,1)} %get-tuple-element.74.mid_ref), channel_id=1, source_target_pairs={{0,1},{1,2},{2,3},{3,4},{4,5},{5,6},{6,7},{7,8},{8,9},{9,10},{10,1... | collective-permute-start | bytes 737288 | tf_op jit(solution)/shard_map/ppermute | solution.py:557
  156.5 3.9 %collective-permute-done.9.refs_1_ = bf16[56,16,256]{2,1,0:T(8,128)(2,1)} collective-permute-done((bf16[56,16,256]{2,1,0:T(8,128)(2,1)}, bf16[56,16,256]{2,1,0:T(8,128)(2,1)}, u32[]{:S(2)}, u32[]{:S(2)}) %collective-permute-start.9) | collective-permute-done | bytes 458784 | tf_op jit(solution)/shard_map/ppermute | solution.py:577
  160.4 5.8 %shard_map.94 = bf16[128,32,128]{2,1,0:T(8,128)(2,1)} custom-call(bf16[3,2,256,1280]{3,2,1,0:T(8,128)(2,1)} %shard_map.89.at_ref, bf16[8,2,120,128]{3,2,1,0:T(8,128)(2,1)} %copy-done.20, bf16[56,16,256]{2,1,0:T(8,128)(2,1)} %get-tuple-element.64.refs_0_, bf16[56,16,256]{2,1,0:T(8,128)(2,1)} %collective-permute-done.9.refs_1_, ...), custom_call_target="tpu_custom_call" | custom-call | flops 2000000000 | bytes 10485760 | tf_op jit(solution)/shard_map/pallas_call | solution.py:429
  166.2 11.4 %all-to-all-start.4 = ((bf16[128,32,128]{2,1,0:T(8,128)(2,1)}), bf16[128,32,128]{2,1,0:T(8,128)(2,1)S(1)}, u32[]{:S(2)}, u32[]{:S(2)}) async-start(bf16[128,32,128]{2,1,0:T(8,128)(2,1)} %shard_map.94), calls=%async_computation.4 | async-start | bytes 2097152 | tf_op jit(solution)/shard_map/all_to_all | solution.py:647
  177.7 2.3 %copy-done.1 = bf16[4608,512]{1,0:T(8,128)(2,1)S(1)} copy-done((bf16[4608,512]{1,0:T(8,128)(2,1)S(1)}, bf16[4608,512]{1,0:T(8,128)(2,1)}, u32[]{:S(2)}) %copy-start.1) | copy-done | bytes 4718616
  181.1 3.9 %shard_map.95 = bf16[2,120,512]{2,1,0:T(8,128)(2,1)} custom-call(bf16[2,120,512]{2,1,0:T(8,128)(2,1)S(1)} %copy-done.16, bf16[2,120,512]{2,1,0:T(8,128)(2,1)S(1)} %collective-permute-done.12.above_ref, bf16[2,120,512]{2,1,0:T(8,128)(2,1)S(1)} %collective-permute-done.13.below_ref, f32[2,120,512]{2,1,0:T(8,128)S(1)} %copy-done.19, ...), custom_call_target="tpu_custom_call" | custom-call | flops 2000000000 | bytes 8388608 | tf_op jit(solution)/shard_map/pallas_call | solution.py:537
  184.9 12.1 %all-to-all-done.4.terms_ref = bf16[128,32,128]{2,1,0:T(8,128)(2,1)S(1)} async-done(((bf16[128,32,128]{2,1,0:T(8,128)(2,1)}), bf16[128,32,128]{2,1,0:T(8,128)(2,1)S(1)}, u32[]{:S(2)}, u32[]{:S(2)}) %all-to-all-start.4) | async-done | bytes 1048608 | tf_op jit(solution)/shard_map/all_to_all | solution.py:647
  (89 shorter events, 28.0 us)
Async XLA Ops:
  1.7 9.9 %collective-permute-start.1 = (bf16[2,120,512]{2,1,0:T(8,128)(2,1)S(1)}, bf16[2,120,512]{2,1,0:T(8,128)(2,1)S(1)}, u32[]{:S(2)}, u32[]{:S(2)}) collective-permute-start(bf16[2,120,512]{2,1,0:T(8,128)(2,1)S(1)} %fusion.11.act_ref), channel_id=1, source_target_pairs={{1,0},{2,1},{3,2},{4,3},{5,4},{6,5},{7,6},{8,7},{9,8},{10,9},{11,1... | collective-permute-start | bytes 737288 | tf_op jit(solution)/shard_map/ppermute | solution.py:557
  5.1 6.6 %collective-permute-start = (bf16[2,120,512]{2,1,0:T(8,128)(2,1)S(1)}, bf16[2,120,512]{2,1,0:T(8,128)(2,1)S(1)}, u32[]{:S(2)}, u32[]{:S(2)}) collective-permute-start(bf16[2,120,512]{2,1,0:T(8,128)(2,1)S(1)} %fusion.11.act_ref), channel_id=1, source_target_pairs={{0,1},{1,2},{2,3},{3,4},{4,5},{5,6},{6,7},{7,8},{8,9},{9,10},{10,1... | collective-permute-start | bytes 737288 | tf_op jit(solution)/shard_map/ppermute | solution.py:557
  12.4 11.6 %copy-start.3 = (bf16[1536,512]{1,0:T(8,128)(2,1)S(1)}, bf16[1536,512]{1,0:T(8,128)(2,1)}, u32[]{:S(2)}) copy-start(bf16[1536,512]{1,0:T(8,128)(2,1)} %tw_ref.3) | copy-start | bytes 4718596
  12.4 11.6 %copy-start.5 = (bf16[512,512]{1,0:T(8,128)(2,1)S(1)}, bf16[512,512]{1,0:T(8,128)(2,1)}, u32[]{:S(2)}) copy-start(bf16[512,512]{1,0:T(8,128)(2,1)} %ow_ref.1) | copy-start | bytes 1572868
  14.7 9.2 %collective-permute-start.2 = (bf16[2,120,512]{2,1,0:T(8,128)(2,1)S(1)}, bf16[2,120,512]{2,1,0:T(8,128)(2,1)S(1)}, u32[]{:S(2)}, u32[]{:S(2)}) collective-permute-start(bf16[2,120,512]{2,1,0:T(8,128)(2,1)S(1)} %get-tuple-element.83), channel_id=1, source_target_pairs={{0,32},{32,64},{64,96},{1,33},{33,65},{65,97},{2,34},{34,66},{66,9... | collective-permute-start | bytes 737288 | tf_op jit(solution)/shard_map/ppermute | solution.py:557
  27.0 14.3 %copy-start.14 = (bf16[2,120,512]{2,1,0:T(8,128)(2,1)}, bf16[2,120,512]{2,1,0:T(8,128)(2,1)S(1)}, u32[]{:S(2)}) copy-start(bf16[2,120,512]{2,1,0:T(8,128)(2,1)S(1)} %get-tuple-element.42.refs_0_) | copy-start | bytes 737284
  27.0 25.2 %all-to-all-start = ((bf16[32,120,128]{2,1,0:T(8,128)(2,1)}), bf16[32,120,128]{2,1,0:T(8,128)(2,1)S(1)}, u32[]{:S(2)}, u32[]{:S(2)}) async-start(bf16[32,120,128]{2,1,0:T(8,128)(2,1)} %bitcast.17), calls=%async_computation | async-start | bytes 1966080 | tf_op jit(solution)/shard_map/all_to_all | solution.py:616
  35.7 7.0 %collective-permute-start.5 = (bf16[4,120,512]{2,1,0:T(8,128)(2,1)S(1)}, bf16[4,120,512]{2,1,0:T(8,128)(2,1)S(1)}, u32[]{:S(2)}, u32[]{:S(2)}) collective-permute-start(bf16[4,120,512]{2,1,0:T(8,128)(2,1)S(1)} %pad_maximum_fusion.bext_ref.refs_2_), channel_id=1, source_target_pairs={{0,1},{1,0},{2,3},{3,2},{4,5},{5,4},{6,7},{7,6},{8,9},{9,8},{10,11... | collective-permute-start | bytes 1474568 | tf_op jit(solution)/shard_map/ppermute | solution.py:562
  36.7 4.6 %collective-permute-start.4 = (bf16[2,120,512]{2,1,0:T(8,128)(2,1)S(1)}, bf16[2,120,512]{2,1,0:T(8,128)(2,1)S(1)}, u32[]{:S(2)}, u32[]{:S(2)}) collective-permute-start(bf16[2,120,512]{2,1,0:T(8,128)(2,1)S(1)} %get-tuple-element.42.refs_0_), channel_id=1, source_target_pairs={{0,1},{1,0},{2,3},{3,2},{4,5},{5,4},{6,7},{7,6},{8,9},{9,8},{10,11... | collective-permute-start | bytes 737288 | tf_op jit(solution)/shard_map/ppermute | solution.py:562
  38.6 2.7 %collective-permute-start.3 = (bf16[2,120,256]{2,1,0:T(8,128)(2,1)S(1)}, bf16[2,120,256]{2,1,0:T(8,128)(2,1)S(1)}, u32[]{:S(2)}, u32[]{:S(2)}) collective-permute-start(bf16[2,120,256]{2,1,0:T(8,128)(2,1)S(1)} %bitcast.80), channel_id=1, source_target_pairs={{0,1},{1,0},{2,3},{3,2},{4,5},{5,4},{6,7},{7,6},{8,9},{9,8},{10,11... | collective-permute-start | bytes 368648 | tf_op jit(solution)/shard_map/ppermute | solution.py:562
  52.1 52.1 %all-to-all-start.1 = ((bf16[8,4,120,256]{3,2,1,0:T(8,128)(2,1)}), bf16[8,4,120,256]{3,2,1,0:T(8,128)(2,1)S(1)}, u32[]{:S(2)}, u32[]{:S(2)}) async-start(bf16[8,4,120,256]{3,2,1,0:T(8,128)(2,1)} %shard_map.87), calls=%async_computation.1 | async-start | bytes 3932160 | tf_op jit(solution)/shard_map/all_to_all | solution.py:572
  104.2 21.7 %all-to-all-start.2 = ((bf16[32,120,128]{2,1,0:T(8,128)(2,1)}), bf16[32,120,128]{2,1,0:T(8,128)(2,1)S(1)}, u32[]{:S(2)}, u32[]{:S(2)}) async-start(bf16[32,120,128]{2,1,0:T(8,128)(2,1)} %bitcast.76), calls=%async_computation.2 | async-start | bytes 1966080 | tf_op jit(solution)/shard_map/all_to_all | solution.py:626
  130.3 2.3 %collective-permute-start.8 = (bf16[2,120,1024]{2,1,0:T(8,128)(2,1)S(1)}, bf16[2,120,1024]{2,1,0:T(8,128)(2,1)S(1)}, u32[]{:S(2)}, u32[]{:S(2)}) collective-permute-start(bf16[2,120,1024]{2,1,0:T(8,128)(2,1)S(1)} %get-tuple-element.58), channel_id=1, source_target_pairs={{0,1},{1,0},{2,3},{3,2},{4,5},{5,4},{6,7},{7,6},{8,9},{9,8},{10,11... | collective-permute-start | bytes 1474568 | tf_op jit(solution)/shard_map/ppermute | solution.py:562
  130.7 1.8 collective-permute-start.7
  130.9 10.0 %collective-permute-start.6 = (bf16[2,120,512]{2,1,0:T(8,128)(2,1)S(1)}, bf16[2,120,512]{2,1,0:T(8,128)(2,1)S(1)}, u32[]{:S(2)}, u32[]{:S(2)}) collective-permute-start(bf16[2,120,512]{2,1,0:T(8,128)(2,1)S(1)} %get-tuple-element.56.own_ref), channel_id=1, source_target_pairs={{32,0},{64,32},{96,64},{33,1},{65,33},{97,65},{34,2},{66,34},{98,6... | collective-permute-start | bytes 737288 | tf_op jit(solution)/shard_map/ppermute | solution.py:557
  137.2 15.6 %copy-start.6 = (bf16[512,512]{1,0:T(8,128)(2,1)S(1)}, bf16[512,512]{1,0:T(8,128)(2,1)}, u32[]{:S(2)}) copy-start(bf16[512,512]{1,0:T(8,128)(2,1)} %ow_ref.1) | copy-start | bytes 1572868
  137.2 23.2 %collective-permute-start.9 = (bf16[56,16,256]{2,1,0:T(8,128)(2,1)}, bf16[56,16,256]{2,1,0:T(8,128)(2,1)}, u32[]{:S(2)}, u32[]{:S(2)}) collective-permute-start(bf16[56,16,256]{2,1,0:T(8,128)(2,1)} %get-tuple-element.70), channel_id=1, source_target_pairs={{0,8},{1,9},{2,10},{3,11},{4,12},{5,13},{6,14},{7,15},{8,16},{9,17... | collective-permute-start | bytes 1376264 | tf_op jit(solution)/shard_map/ppermute | solution.py:577
  137.3 23.1 %collective-permute-start.10 = (bf16[56,16,256]{2,1,0:T(8,128)(2,1)S(1)}, bf16[56,16,256]{2,1,0:T(8,128)(2,1)}, u32[]{:S(2)}, u32[]{:S(2)}) collective-permute-start(bf16[56,16,256]{2,1,0:T(8,128)(2,1)S(1)} %get-tuple-element.71), channel_id=1, source_target_pairs={{0,16},{1,17},{2,18},{3,19},{4,20},{5,21},{6,22},{7,23},{8,24},{9,... | collective-permute-start | bytes 1376264 | tf_op jit(solution)/shard_map/ppermute | solution.py:577
  139.0 21.5 %collective-permute-start.11 = (bf16[56,16,256]{2,1,0:T(8,128)(2,1)S(1)}, bf16[56,16,256]{2,1,0:T(8,128)(2,1)}, u32[]{:S(2)}, u32[]{:S(2)}) collective-permute-start(bf16[56,16,256]{2,1,0:T(8,128)(2,1)S(1)} %get-tuple-element.72), channel_id=1, source_target_pairs={{0,24},{1,25},{2,26},{3,27},{4,28},{5,29},{6,30},{7,31},{8,0},{9,1... | collective-permute-start | bytes 1376264 | tf_op jit(solution)/shard_map/ppermute | solution.py:577
  142.9 13.6 %all-to-all-start.3 = ((bf16[8,2,120,128]{3,2,1,0:T(8,128)(2,1)}), bf16[8,2,120,128]{3,2,1,0:T(8,128)(2,1)S(1)}, u32[]{:S(2)}, u32[]{:S(2)}) async-start(bf16[8,2,120,128]{3,2,1,0:T(8,128)(2,1)} %get-tuple-element.66), calls=%async_computation.3 | async-start | bytes 983040 | tf_op jit(solution)/shard_map/all_to_all | solution.py:572
  147.2 19.0 %collective-permute-start.13 = (bf16[2,120,512]{2,1,0:T(8,128)(2,1)}, bf16[2,120,512]{2,1,0:T(8,128)(2,1)S(1)}, u32[]{:S(2)}, u32[]{:S(2)}) collective-permute-start(bf16[2,120,512]{2,1,0:T(8,128)(2,1)} %get-tuple-element.74.mid_ref), channel_id=1, source_target_pairs={{1,0},{2,1},{3,2},{4,3},{5,4},{6,5},{7,6},{8,7},{9,8},{10,9},{11,1... | collective-permute-start | bytes 737288 | tf_op jit(solution)/shard_map/ppermute | solution.py:557
  149.2 17.0 %collective-permute-start.12 = (bf16[2,120,512]{2,1,0:T(8,128)(2,1)}, bf16[2,120,512]{2,1,0:T(8,128)(2,1)S(1)}, u32[]{:S(2)}, u32[]{:S(2)}) collective-permute-start(bf16[2,120,512]{2,1,0:T(8,128)(2,1)} %get-tuple-element.74.mid_ref), channel_id=1, source_target_pairs={{0,1},{1,2},{2,3},{3,4},{4,5},{5,6},{6,7},{7,8},{8,9},{9,10},{10,1... | collective-permute-start | bytes 737288 | tf_op jit(solution)/shard_map/ppermute | solution.py:557
  156.5 21.2 %copy-start.16 = (bf16[2,120,512]{2,1,0:T(8,128)(2,1)S(1)}, bf16[2,120,512]{2,1,0:T(8,128)(2,1)}, u32[]{:S(2)}) copy-start(bf16[2,120,512]{2,1,0:T(8,128)(2,1)} %get-tuple-element.74.mid_ref) | copy-start | bytes 737284
  166.2 30.8 %all-to-all-start.4 = ((bf16[128,32,128]{2,1,0:T(8,128)(2,1)}), bf16[128,32,128]{2,1,0:T(8,128)(2,1)S(1)}, u32[]{:S(2)}, u32[]{:S(2)}) async-start(bf16[128,32,128]{2,1,0:T(8,128)(2,1)} %shard_map.94), calls=%async_computation.4 | async-start | bytes 2097152 | tf_op jit(solution)/shard_map/all_to_all | solution.py:647
  (17 other events, 76.7 us)

commit v2 on v1

--- a/solution.py
+++ b/solution.py
@@ -313,18 +313,13 @@
     near, (at_ref, pay_ref, cot_ref, mix_ref, out_ref, sems) = scratch[:5], scratch[5:]
     rt_ref, bt_ref, p0_ref, c0_ref, c1_ref = near
     copies = [pltpu.make_async_copy(src, dst, sems.at[k]) for k, (src, dst) in enumerate(zip(far, near))]
-    for copy in copies:
-        copy.start()
-    for copy in copies:
-        copy.wait()
+    for at in (3, 4, 2, 0, 1):
+        copies[at].start()
     frames, width, chans = a0_ref.shape
     half = chans // 2
-    for d, (a, p, c) in enumerate(((a0_ref, p0_ref, c0_ref), (a1_ref, p1_ref, c1_ref))):
-        for f in range(frames):
-            at = (d * frames + f) * LANES
-            at_ref[:, at : at + LANES] = padded(a[f]).T.astype(BF)
-            pay_ref[at : at + LANES, :] = padded(p[f]).astype(BF)
-            cot_ref[at : at + LANES, :] = padded(c[f]).astype(BF)
+    places = [(d, f, (d * frames + f) * LANES) for d in range(2) for f in range(frames)]
+    for d, f, at in places:
+        at_ref[:, at : at + LANES] = padded((a0_ref, a1_ref)[d][f]).T.astype(BF)
     parts, _, rows, _ = out_ref.shape
     block = parts * rows
 
@@ -334,6 +329,23 @@
                 at = n * block + y * rows
                 out_ref[y, first + n, :, lane : lane + value.shape[1]] = value[at : at + rows].astype(BF)
 
+    copies[3].wait()
+    copies[4].wait()
+    for d, f, at in places:
+        cot_ref[at : at + LANES, :] = padded((c0_ref, c1_ref)[d][f]).astype(BF)
+    put(6 * chans // block, jnp.dot(at_ref[...], cot_ref[...], preferred_element_type=F32))
+    copies[2].wait()
+    for d, f, at in places:
+        pay_ref[at : at + LANES, :] = padded((p0_ref, p1_ref)[d][f]).astype(BF)
+    copies[0].wait()
+    for p in range(3):
+        right = pay_ref[:, p * half : (p + 1) * half]
+        for lane in range(0, half, LANES):
+            value = jnp.dot(rt_ref[...], right[:, lane : lane + LANES], preferred_element_type=F32)
+            mix_ref[lane // LANES, pl.ds(p, chans, stride=3), :] = value
+    for lane in range(0, half, LANES):
+        put(3 * chans // block, mix_ref[lane // LANES], lane)
+    copies[1].wait()
     for k in range(3):
         acc = jnp.zeros((chans, half), F32)
         for d in range(2):
@@ -341,14 +353,6 @@
             right = pay_ref[d * frames * LANES : (d + 1) * frames * LANES, 3 * half :]
             acc = acc + jnp.dot(left, right, preferred_element_type=F32)
         put(k * chans // block, acc)
-    for p in range(3):
-        right = pay_ref[:, p * half : (p + 1) * half]
-        for lane in range(0, half, LANES):
-            value = jnp.dot(rt_ref[...], right[:, lane : lane + LANES], preferred_element_type=F32)
-            mix_ref[lane // LANES, pl.ds(p, chans, stride=3), :] = value
-    for lane in range(0, half, LANES):
-        put(3 * chans // block, mix_ref[lane // LANES], lane)
-    put(6 * chans // block, jnp.dot(at_ref[...], cot_ref[...], preferred_element_type=F32))
     for k, out in enumerate(outs):
         out[...] = out_ref[lax.rem(line_ref[0] + k, parts)]
 
@@ -638,7 +642,7 @@
     dpre, near = make_dpre(dresb, dnext, slope, temporal_weight)
     near = exchange(near)
     dabove, dbelow = neighbours(dpre)
-    parts = [local[0]] + [along_y(local[by], by) for by in range(1, 4)]
+    parts = [along_y(local[by], by) for by in (2, 1, 3)] + [local[0]]
     mixed = resid.reshape(ntok, chans) + matmul(atted.reshape(ntok, chans), out_weight)
     mixed = mixed.astype(BF).reshape(latents.shape)
     mixed, near = lax.optimization_barrier((mixed, near))

time: 199 us -> 199 us (level)
  transfers between devices with their start and end apart: 19 -> 19, of which waited for: 9 -> 7; matrix products, arithmetic and copies ran while one was open for 3% -> 3% of each run, Pallas kernels for 36% -> 36%
where the time goes in v2:
time: 199 us; the launch traced here: 198 us
  Pallas kernels  79.1 us (40%)
  starting transfers between devices  54.8 us (28%)
  waiting for transfers between devices  45.1 us (23%)
  local copies, waits for them, and re-layouts  11.8 us (6%)
  matrix products  4.31 us (2%)
    pallas_call x1, Pallas kernels, attn(): pl.pallas_call(functools.partial(attn_kernel, 1.0 / math.sqrt(32), tq, ck...  48.2 us
    ppermute x6, starting transfers between devices, shift(): return lax.ppermute(x, axis, pairs)  16.8 us
    all_to_all x1, waiting for transfers between devices, per_device(): terms = lax.all_to_all(terms, ('tm', 'space'), 0, 0, tiled=True)  12.1 us
    all_to_all x1, waiting for transfers between devices, per_device(): outs = lax.all_to_all(outs, 'space', 0, 0, tiled=True)  11.7 us
    all_to_all x1, starting transfers between devices, per_device(): terms = lax.all_to_all(terms, ('tm', 'space'), 0, 0, tiled=True)  10.6 us
    unnamed x52, local copies, waits for them, and re-layouts  9.4 us
    all_to_all x1, starting transfers between devices, per_device(): items = lax.all_to_all(items, 'space', 0, 0, tiled=True)  8.7 us
    all_to_all x1, waiting for transfers between devices, per_device(): items = lax.all_to_all(items, 'space', 0, 0, tiled=True)  8.7 us
  transfers between devices with their start and end apart: 19, of which 7 were waited for; matrix products, arithmetic and copies ran while one was open for 3% of the time, Pallas kernels for 36%

profile of v2, /device:TPU:1, one launch (start us, length us, event | category | flops | bytes accessed | tf_op | source)
XLA Modules:
  0.0 197.9 jit_solution(9379273228728166642)
XLA Ops:
  1.7 3.3 %collective-permute-start.1 = (bf16[2,120,512]{2,1,0:T(8,128)(2,1)S(1)}, bf16[2,120,512]{2,1,0:T(8,128)(2,1)S(1)}, u32[]{:S(2)}, u32[]{:S(2)}) collective-permute-start(bf16[2,120,512]{2,1,0:T(8,128)(2,1)S(1)} %fusion.11.act_ref), channel_id=1, source_target_pairs={{1,0},{2,1},{3,2},{4,3},{5,4},{6,5},{7,6},{8,7},{9,8},{10,9},{11,1... | collective-permute-start | bytes 737288 | tf_op jit(solution)/shard_map/ppermute | solution.py:561
  5.1 3.1 %collective-permute-start = (bf16[2,120,512]{2,1,0:T(8,128)(2,1)S(1)}, bf16[2,120,512]{2,1,0:T(8,128)(2,1)S(1)}, u32[]{:S(2)}, u32[]{:S(2)}) collective-permute-start(bf16[2,120,512]{2,1,0:T(8,128)(2,1)S(1)} %fusion.11.act_ref), channel_id=1, source_target_pairs={{0,1},{1,2},{2,3},{3,4},{4,5},{5,6},{6,7},{7,8},{8,9},{9,10},{10,1... | collective-permute-start | bytes 737288 | tf_op jit(solution)/shard_map/ppermute | solution.py:561
  8.2 2.3 %copy-done = bf16[4608,512]{1,0:T(8,128)(2,1)S(1)} copy-done((bf16[4608,512]{1,0:T(8,128)(2,1)S(1)}, bf16[4608,512]{1,0:T(8,128)(2,1)}, u32[]{:S(2)}) %copy-start) | copy-done | bytes 4718616
  14.7 3.5 %collective-permute-start.2 = (bf16[2,120,512]{2,1,0:T(8,128)(2,1)S(1)}, bf16[2,120,512]{2,1,0:T(8,128)(2,1)S(1)}, u32[]{:S(2)}, u32[]{:S(2)}) collective-permute-start(bf16[2,120,512]{2,1,0:T(8,128)(2,1)S(1)} %get-tuple-element.83), channel_id=1, source_target_pairs={{0,32},{32,64},{64,96},{1,33},{33,65},{65,97},{2,34},{34,66},{66,9... | collective-permute-start | bytes 737288 | tf_op jit(solution)/shard_map/ppermute | solution.py:561
  18.3 5.7 %collective-permute-done.2 = bf16[2,120,512]{2,1,0:T(8,128)(2,1)S(1)} collective-permute-done((bf16[2,120,512]{2,1,0:T(8,128)(2,1)S(1)}, bf16[2,120,512]{2,1,0:T(8,128)(2,1)S(1)}, u32[]{:S(2)}, u32[]{:S(2)}) %collective-permute-start.2) | collective-permute-done | bytes 245792 | tf_op jit(solution)/shard_map/ppermute | solution.py:561
  24.1 2.9 %shard_map.86 = (f32[2,120,512]{2,1,0:T(8,128)}, bf16[2,120,512]{2,1,0:T(8,128)(2,1)S(1)}, bf16[2,16,120,128]{3,2,1,0:T(8,128)(2,1)}) custom-call(bf16[2,120,512]{2,1,0:T(8,128)(2,1)S(1)} %bitcast.68, bf16[4,120,512]{2,1,0:T(8,128)(2,1)S(1)} %pad_maximum_fusion.bext_ref.refs_2_, bf16[2,120,512]{2,1,0:T(8,128)(2,1)S(1)} %bitcast.72, ...), custom_call_target="tpu_custom_call" | custom-call | flops 2000000000 | bytes 6291456 | tf_op jit(solution)/shard_map/pallas_call | solution.py:42
  27.0 8.7 %all-to-all-start = ((bf16[32,120,128]{2,1,0:T(8,128)(2,1)}), bf16[32,120,128]{2,1,0:T(8,128)(2,1)S(1)}, u32[]{:S(2)}, u32[]{:S(2)}) async-start(bf16[32,120,128]{2,1,0:T(8,128)(2,1)} %bitcast.17), calls=%async_computation | async-start | bytes 1966080 | tf_op jit(solution)/shard_map/all_to_all | solution.py:620
  43.4 8.7 %all-to-all-done = bf16[32,120,128]{2,1,0:T(8,128)(2,1)S(1)} async-done(((bf16[32,120,128]{2,1,0:T(8,128)(2,1)}), bf16[32,120,128]{2,1,0:T(8,128)(2,1)S(1)}, u32[]{:S(2)}, u32[]{:S(2)}) %all-to-all-start) | async-done | bytes 983072 | tf_op jit(solution)/shard_map/all_to_all | solution.py:620
  52.1 3.9 %all-to-all-start.1 = ((bf16[8,4,120,256]{3,2,1,0:T(8,128)(2,1)}), bf16[8,4,120,256]{3,2,1,0:T(8,128)(2,1)S(1)}, u32[]{:S(2)}, u32[]{:S(2)}) async-start(bf16[8,4,120,256]{3,2,1,0:T(8,128)(2,1)} %shard_map.87), calls=%async_computation.1 | async-start | bytes 3932160 | tf_op jit(solution)/shard_map/all_to_all | solution.py:576
  56.0 48.2 %shard_map.88 = bf16[3840,128]{1,0:T(8,128)(2,1)} custom-call(bf16[3840,128]{1,0:T(8,128)(2,1)S(1)} %bitcast.70), custom_call_target="tpu_custom_call" | custom-call | flops 22649241600 | bytes 1966080 | tf_op jit(solution)/shard_map/pallas_call | solution.py:212
  104.2 5.2 %all-to-all-start.2 = ((bf16[32,120,128]{2,1,0:T(8,128)(2,1)}), bf16[32,120,128]{2,1,0:T(8,128)(2,1)S(1)}, u32[]{:S(2)}, u32[]{:S(2)}) async-start(bf16[32,120,128]{2,1,0:T(8,128)(2,1)} %bitcast.76), calls=%async_computation.2 | async-start | bytes 1966080 | tf_op jit(solution)/shard_map/all_to_all | solution.py:630
  109.5 3.1 %shard_map.89.at_ref = bf16[3,2,256,1280]{3,2,1,0:T(8,128)(2,1)} custom-call(bf16[8,4,120,256]{3,2,1,0:T(8,128)(2,1)S(1)} %all-to-all-done.1.r_ref), custom_call_target="tpu_custom_call" | custom-call | flops 1000000000 | bytes 6291456 | tf_op jit(solution)/shard_map/pallas_call | solution.py:281
  114.2 11.7 %all-to-all-done.2 = bf16[32,120,128]{2,1,0:T(8,128)(2,1)S(1)} async-done(((bf16[32,120,128]{2,1,0:T(8,128)(2,1)}), bf16[32,120,128]{2,1,0:T(8,128)(2,1)S(1)}, u32[]{:S(2)}, u32[]{:S(2)}) %all-to-all-start.2) | async-done | bytes 983072 | tf_op jit(solution)/shard_map/all_to_all | solution.py:630
  125.9 4.3 %shard_map.91 = (bf16[2,120,512]{2,1,0:T(8,128)(2,1)S(1)}, f32[2,120,512]{2,1,0:T(8,128)}, bf16[2,120,512]{2,1,0:T(8,128)(2,1)S(1)}, bf16[2,120,1024]{2,1,0:T(8,128)(2,1)}, bf16[2,120,1024]{2,1,0:T(8,128)(2,1)S(1)}) custom-call(s32[1]{0:T(128)} %bitcast.14.core_ref, bf16[2,16,120,128]{3,2,1,0:T(8,128)(2,1)S(1)} %bitcast.71, ...), custom_call_target="tpu_custom_call" | custom-call | flops 1000000000 | bytes 6291456 | tf_op jit(solution)/shard_map/pallas_call | solution.py:103
  132.6 4.5 %shard_map.92 = (bf16[56,16,256]{2,1,0:T(8,128)(2,1)}, bf16[56,16,256]{2,1,0:T(8,128)(2,1)S(1)}, bf16[56,16,256]{2,1,0:T(8,128)(2,1)}, bf16[56,16,256]{2,1,0:T(8,128)(2,1)S(1)}) custom-call(s32[1]{0:T(128)} %bitcast.23.line_ref, bf16[2,120,512]{2,1,0:T(8,128)(2,1)S(1)} %get-tuple-element.55.a0_ref, bf16[2,120,512]{2,1,0:T(8,128)(2,1)S(1)} %collective-permute-done.7.a1_ref, ...), custom_call_target="tpu_custom_call" | custom-call | flops 2000000000 | bytes 10485760 | tf_op jit(solution)/shard_map/pallas_call | solution.py:366
  138.3 2.6 %collective-permute-start.11 = (bf16[56,16,256]{2,1,0:T(8,128)(2,1)S(1)}, bf16[56,16,256]{2,1,0:T(8,128)(2,1)}, u32[]{:S(2)}, u32[]{:S(2)}) collective-permute-start(bf16[56,16,256]{2,1,0:T(8,128)(2,1)S(1)} %get-tuple-element.72), channel_id=1, source_target_pairs={{0,24},{1,25},{2,26},{3,27},{4,28},{5,29},{6,30},{7,31},{8,0},{9,1... | collective-permute-start | bytes 1376264 | tf_op jit(solution)/shard_map/ppermute | solution.py:581
  142.9 4.4 %all-to-all-start.3 = ((bf16[8,2,120,128]{3,2,1,0:T(8,128)(2,1)}), bf16[8,2,120,128]{3,2,1,0:T(8,128)(2,1)S(1)}, u32[]{:S(2)}, u32[]{:S(2)}) async-start(bf16[8,2,120,128]{3,2,1,0:T(8,128)(2,1)} %get-tuple-element.66), calls=%async_computation.3 | async-start | bytes 983040 | tf_op jit(solution)/shard_map/all_to_all | solution.py:576
  149.3 3.5 %collective-permute-start.12 = (bf16[2,120,512]{2,1,0:T(8,128)(2,1)}, bf16[2,120,512]{2,1,0:T(8,128)(2,1)S(1)}, u32[]{:S(2)}, u32[]{:S(2)}) collective-permute-start(bf16[2,120,512]{2,1,0:T(8,128)(2,1)} %get-tuple-element.74.mid_ref), channel_id=1, source_target_pairs={{0,1},{1,2},{2,3},{3,4},{4,5},{5,6},{6,7},{7,8},{8,9},{9,10},{10,1... | collective-permute-start | bytes 737288 | tf_op jit(solution)/shard_map/ppermute | solution.py:561
  156.4 4.9 %collective-permute-done.10.refs_1_ = bf16[56,16,256]{2,1,0:T(8,128)(2,1)} collective-permute-done((bf16[56,16,256]{2,1,0:T(8,128)(2,1)S(1)}, bf16[56,16,256]{2,1,0:T(8,128)(2,1)}, u32[]{:S(2)}, u32[]{:S(2)}) %collective-permute-start.10) | collective-permute-done | bytes 458784 | tf_op jit(solution)/shard_map/ppermute | solution.py:581
  161.3 5.8 %shard_map.94 = bf16[128,32,128]{2,1,0:T(8,128)(2,1)} custom-call(bf16[3,2,256,1280]{3,2,1,0:T(8,128)(2,1)} %shard_map.89.at_ref, bf16[8,2,120,128]{3,2,1,0:T(8,128)(2,1)} %copy-done.20, bf16[56,16,256]{2,1,0:T(8,128)(2,1)} %collective-permute-done.9.refs_0_, bf16[56,16,256]{2,1,0:T(8,128)(2,1)} %collective-permute-done.10.refs_1_, ...), custom_call_target="tpu_custom_call" | custom-call | flops 2000000000 | bytes 10485760 | tf_op jit(solution)/shard_map/pallas_call | solution.py:433
  167.1 10.6 %all-to-all-start.4 = ((bf16[128,32,128]{2,1,0:T(8,128)(2,1)}), bf16[128,32,128]{2,1,0:T(8,128)(2,1)S(1)}, u32[]{:S(2)}, u32[]{:S(2)}) async-start(bf16[128,32,128]{2,1,0:T(8,128)(2,1)} %shard_map.94), calls=%async_computation.4 | async-start | bytes 2097152 | tf_op jit(solution)/shard_map/all_to_all | solution.py:651
  177.7 2.3 %copy-done.1 = bf16[4608,512]{1,0:T(8,128)(2,1)S(1)} copy-done((bf16[4608,512]{1,0:T(8,128)(2,1)S(1)}, bf16[4608,512]{1,0:T(8,128)(2,1)}, u32[]{:S(2)}) %copy-start.1) | copy-done | bytes 4718616
  181.1 3.9 %shard_map.95 = bf16[2,120,512]{2,1,0:T(8,128)(2,1)} custom-call(bf16[2,120,512]{2,1,0:T(8,128)(2,1)S(1)} %copy-done.16, bf16[2,120,512]{2,1,0:T(8,128)(2,1)S(1)} %collective-permute-done.12.above_ref, bf16[2,120,512]{2,1,0:T(8,128)(2,1)S(1)} %collective-permute-done.13.below_ref, f32[2,120,512]{2,1,0:T(8,128)S(1)} %copy-done.19, ...), custom_call_target="tpu_custom_call" | custom-call | flops 2000000000 | bytes 8388608 | tf_op jit(solution)/shard_map/pallas_call | solution.py:541
  185.0 12.1 %all-to-all-done.4.terms_ref = bf16[128,32,128]{2,1,0:T(8,128)(2,1)S(1)} async-done(((bf16[128,32,128]{2,1,0:T(8,128)(2,1)}), bf16[128,32,128]{2,1,0:T(8,128)(2,1)S(1)}, u32[]{:S(2)}, u32[]{:S(2)}) %all-to-all-start.4) | async-done | bytes 1048608 | tf_op jit(solution)/shard_map/all_to_all | solution.py:651
  (89 shorter events, 27.6 us)
Async XLA Ops:
  1.7 9.9 %collective-permute-start.1 = (bf16[2,120,512]{2,1,0:T(8,128)(2,1)S(1)}, bf16[2,120,512]{2,1,0:T(8,128)(2,1)S(1)}, u32[]{:S(2)}, u32[]{:S(2)}) collective-permute-start(bf16[2,120,512]{2,1,0:T(8,128)(2,1)S(1)} %fusion.11.act_ref), channel_id=1, source_target_pairs={{1,0},{2,1},{3,2},{4,3},{5,4},{6,5},{7,6},{8,7},{9,8},{10,9},{11,1... | collective-permute-start | bytes 737288 | tf_op jit(solution)/shard_map/ppermute | solution.py:561
  5.1 6.6 %collective-permute-start = (bf16[2,120,512]{2,1,0:T(8,128)(2,1)S(1)}, bf16[2,120,512]{2,1,0:T(8,128)(2,1)S(1)}, u32[]{:S(2)}, u32[]{:S(2)}) collective-permute-start(bf16[2,120,512]{2,1,0:T(8,128)(2,1)S(1)} %fusion.11.act_ref), channel_id=1, source_target_pairs={{0,1},{1,2},{2,3},{3,4},{4,5},{5,6},{6,7},{7,8},{8,9},{9,10},{10,1... | collective-permute-start | bytes 737288 | tf_op jit(solution)/shard_map/ppermute | solution.py:561
  12.4 11.6 %copy-start.3 = (bf16[1536,512]{1,0:T(8,128)(2,1)S(1)}, bf16[1536,512]{1,0:T(8,128)(2,1)}, u32[]{:S(2)}) copy-start(bf16[1536,512]{1,0:T(8,128)(2,1)} %tw_ref.3) | copy-start | bytes 4718596
  12.4 11.6 %copy-start.5 = (bf16[512,512]{1,0:T(8,128)(2,1)S(1)}, bf16[512,512]{1,0:T(8,128)(2,1)}, u32[]{:S(2)}) copy-start(bf16[512,512]{1,0:T(8,128)(2,1)} %ow_ref.1) | copy-start | bytes 1572868
  14.7 9.2 %collective-permute-start.2 = (bf16[2,120,512]{2,1,0:T(8,128)(2,1)S(1)}, bf16[2,120,512]{2,1,0:T(8,128)(2,1)S(1)}, u32[]{:S(2)}, u32[]{:S(2)}) collective-permute-start(bf16[2,120,512]{2,1,0:T(8,128)(2,1)S(1)} %get-tuple-element.83), channel_id=1, source_target_pairs={{0,32},{32,64},{64,96},{1,33},{33,65},{65,97},{2,34},{34,66},{66,9... | collective-permute-start | bytes 737288 | tf_op jit(solution)/shard_map/ppermute | solution.py:561
  27.0 14.3 %copy-start.14 = (bf16[2,120,512]{2,1,0:T(8,128)(2,1)}, bf16[2,120,512]{2,1,0:T(8,128)(2,1)S(1)}, u32[]{:S(2)}) copy-start(bf16[2,120,512]{2,1,0:T(8,128)(2,1)S(1)} %get-tuple-element.42.refs_0_) | copy-start | bytes 737284
  27.0 25.2 %all-to-all-start = ((bf16[32,120,128]{2,1,0:T(8,128)(2,1)}), bf16[32,120,128]{2,1,0:T(8,128)(2,1)S(1)}, u32[]{:S(2)}, u32[]{:S(2)}) async-start(bf16[32,120,128]{2,1,0:T(8,128)(2,1)} %bitcast.17), calls=%async_computation | async-start | bytes 1966080 | tf_op jit(solution)/shard_map/all_to_all | solution.py:620
  35.7 7.0 %collective-permute-start.5 = (bf16[4,120,512]{2,1,0:T(8,128)(2,1)S(1)}, bf16[4,120,512]{2,1,0:T(8,128)(2,1)S(1)}, u32[]{:S(2)}, u32[]{:S(2)}) collective-permute-start(bf16[4,120,512]{2,1,0:T(8,128)(2,1)S(1)} %pad_maximum_fusion.bext_ref.refs_2_), channel_id=1, source_target_pairs={{0,1},{1,0},{2,3},{3,2},{4,5},{5,4},{6,7},{7,6},{8,9},{9,8},{10,11... | collective-permute-start | bytes 1474568 | tf_op jit(solution)/shard_map/ppermute | solution.py:566
  36.7 4.6 %collective-permute-start.4 = (bf16[2,120,512]{2,1,0:T(8,128)(2,1)S(1)}, bf16[2,120,512]{2,1,0:T(8,128)(2,1)S(1)}, u32[]{:S(2)}, u32[]{:S(2)}) collective-permute-start(bf16[2,120,512]{2,1,0:T(8,128)(2,1)S(1)} %get-tuple-element.42.refs_0_), channel_id=1, source_target_pairs={{0,1},{1,0},{2,3},{3,2},{4,5},{5,4},{6,7},{7,6},{8,9},{9,8},{10,11... | collective-permute-start | bytes 737288 | tf_op jit(solution)/shard_map/ppermute | solution.py:566
  38.6 2.7 %collective-permute-start.3 = (bf16[2,120,256]{2,1,0:T(8,128)(2,1)S(1)}, bf16[2,120,256]{2,1,0:T(8,128)(2,1)S(1)}, u32[]{:S(2)}, u32[]{:S(2)}) collective-permute-start(bf16[2,120,256]{2,1,0:T(8,128)(2,1)S(1)} %bitcast.80), channel_id=1, source_target_pairs={{0,1},{1,0},{2,3},{3,2},{4,5},{5,4},{6,7},{7,6},{8,9},{9,8},{10,11... | collective-permute-start | bytes 368648 | tf_op jit(solution)/shard_map/ppermute | solution.py:566
  52.1 52.1 %all-to-all-start.1 = ((bf16[8,4,120,256]{3,2,1,0:T(8,128)(2,1)}), bf16[8,4,120,256]{3,2,1,0:T(8,128)(2,1)S(1)}, u32[]{:S(2)}, u32[]{:S(2)}) async-start(bf16[8,4,120,256]{3,2,1,0:T(8,128)(2,1)} %shard_map.87), calls=%async_computation.1 | async-start | bytes 3932160 | tf_op jit(solution)/shard_map/all_to_all | solution.py:576
  104.2 21.7 %all-to-all-start.2 = ((bf16[32,120,128]{2,1,0:T(8,128)(2,1)}), bf16[32,120,128]{2,1,0:T(8,128)(2,1)S(1)}, u32[]{:S(2)}, u32[]{:S(2)}) async-start(bf16[32,120,128]{2,1,0:T(8,128)(2,1)} %bitcast.76), calls=%async_computation.2 | async-start | bytes 1966080 | tf_op jit(solution)/shard_map/all_to_all | solution.py:630
  130.3 2.3 %collective-permute-start.8 = (bf16[2,120,1024]{2,1,0:T(8,128)(2,1)S(1)}, bf16[2,120,1024]{2,1,0:T(8,128)(2,1)S(1)}, u32[]{:S(2)}, u32[]{:S(2)}) collective-permute-start(bf16[2,120,1024]{2,1,0:T(8,128)(2,1)S(1)} %get-tuple-element.58), channel_id=1, source_target_pairs={{0,1},{1,0},{2,3},{3,2},{4,5},{5,4},{6,7},{7,6},{8,9},{9,8},{10,11... | collective-permute-start | bytes 1474568 | tf_op jit(solution)/shard_map/ppermute | solution.py:566
  130.7 1.8 collective-permute-start.7
  130.9 10.0 %collective-permute-start.6 = (bf16[2,120,512]{2,1,0:T(8,128)(2,1)S(1)}, bf16[2,120,512]{2,1,0:T(8,128)(2,1)S(1)}, u32[]{:S(2)}, u32[]{:S(2)}) collective-permute-start(bf16[2,120,512]{2,1,0:T(8,128)(2,1)S(1)} %get-tuple-element.56.own_ref), channel_id=1, source_target_pairs={{32,0},{64,32},{96,64},{33,1},{65,33},{97,65},{34,2},{66,34},{98,6... | collective-permute-start | bytes 737288 | tf_op jit(solution)/shard_map/ppermute | solution.py:561
  137.1 15.7 %copy-start.6 = (bf16[512,512]{1,0:T(8,128)(2,1)S(1)}, bf16[512,512]{1,0:T(8,128)(2,1)}, u32[]{:S(2)}) copy-start(bf16[512,512]{1,0:T(8,128)(2,1)} %ow_ref.1) | copy-start | bytes 1572868
  137.1 19.3 %collective-permute-start.9 = (bf16[56,16,256]{2,1,0:T(8,128)(2,1)}, bf16[56,16,256]{2,1,0:T(8,128)(2,1)}, u32[]{:S(2)}, u32[]{:S(2)}) collective-permute-start(bf16[56,16,256]{2,1,0:T(8,128)(2,1)} %get-tuple-element.70), channel_id=1, source_target_pairs={{0,16},{1,17},{2,18},{3,19},{4,20},{5,21},{6,22},{7,23},{8,24},{9,... | collective-permute-start | bytes 1376264 | tf_op jit(solution)/shard_map/ppermute | solution.py:581
  138.2 23.1 %collective-permute-start.10 = (bf16[56,16,256]{2,1,0:T(8,128)(2,1)S(1)}, bf16[56,16,256]{2,1,0:T(8,128)(2,1)}, u32[]{:S(2)}, u32[]{:S(2)}) collective-permute-start(bf16[56,16,256]{2,1,0:T(8,128)(2,1)S(1)} %get-tuple-element.71), channel_id=1, source_target_pairs={{0,8},{1,9},{2,10},{3,11},{4,12},{5,13},{6,14},{7,15},{8,16},{9,17... | collective-permute-start | bytes 1376264 | tf_op jit(solution)/shard_map/ppermute | solution.py:581
  138.3 23.0 %collective-permute-start.11 = (bf16[56,16,256]{2,1,0:T(8,128)(2,1)S(1)}, bf16[56,16,256]{2,1,0:T(8,128)(2,1)}, u32[]{:S(2)}, u32[]{:S(2)}) collective-permute-start(bf16[56,16,256]{2,1,0:T(8,128)(2,1)S(1)} %get-tuple-element.72), channel_id=1, source_target_pairs={{0,24},{1,25},{2,26},{3,27},{4,28},{5,29},{6,30},{7,31},{8,0},{9,1... | collective-permute-start | bytes 1376264 | tf_op jit(solution)/shard_map/ppermute | solution.py:581
  142.9 13.5 %all-to-all-start.3 = ((bf16[8,2,120,128]{3,2,1,0:T(8,128)(2,1)}), bf16[8,2,120,128]{3,2,1,0:T(8,128)(2,1)S(1)}, u32[]{:S(2)}, u32[]{:S(2)}) async-start(bf16[8,2,120,128]{3,2,1,0:T(8,128)(2,1)} %get-tuple-element.66), calls=%async_computation.3 | async-start | bytes 983040 | tf_op jit(solution)/shard_map/all_to_all | solution.py:576
  147.3 19.8 %collective-permute-start.13 = (bf16[2,120,512]{2,1,0:T(8,128)(2,1)}, bf16[2,120,512]{2,1,0:T(8,128)(2,1)S(1)}, u32[]{:S(2)}, u32[]{:S(2)}) collective-permute-start(bf16[2,120,512]{2,1,0:T(8,128)(2,1)} %get-tuple-element.74.mid_ref), channel_id=1, source_target_pairs={{1,0},{2,1},{3,2},{4,3},{5,4},{6,5},{7,6},{8,7},{9,8},{10,9},{11,1... | collective-permute-start | bytes 737288 | tf_op jit(solution)/shard_map/ppermute | solution.py:561
  149.3 17.8 %collective-permute-start.12 = (bf16[2,120,512]{2,1,0:T(8,128)(2,1)}, bf16[2,120,512]{2,1,0:T(8,128)(2,1)S(1)}, u32[]{:S(2)}, u32[]{:S(2)}) collective-permute-start(bf16[2,120,512]{2,1,0:T(8,128)(2,1)} %get-tuple-element.74.mid_ref), channel_id=1, source_target_pairs={{0,1},{1,2},{2,3},{3,4},{4,5},{5,6},{6,7},{7,8},{8,9},{9,10},{10,1... | collective-permute-start | bytes 737288 | tf_op jit(solution)/shard_map/ppermute | solution.py:561
  156.4 21.3 %copy-start.16 = (bf16[2,120,512]{2,1,0:T(8,128)(2,1)S(1)}, bf16[2,120,512]{2,1,0:T(8,128)(2,1)}, u32[]{:S(2)}) copy-start(bf16[2,120,512]{2,1,0:T(8,128)(2,1)} %get-tuple-element.74.mid_ref) | copy-start | bytes 737284
  167.1 30.0 %all-to-all-start.4 = ((bf16[128,32,128]{2,1,0:T(8,128)(2,1)}), bf16[128,32,128]{2,1,0:T(8,128)(2,1)S(1)}, u32[]{:S(2)}, u32[]{:S(2)}) async-start(bf16[128,32,128]{2,1,0:T(8,128)(2,1)} %shard_map.94), calls=%async_computation.4 | async-start | bytes 2097152 | tf_op jit(solution)/shard_map/all_to_all | solution.py:651
  (17 other events, 77.6 us)

commit v3 on v2

--- a/solution.py
+++ b/solution.py
@@ -611,7 +611,7 @@
     cot = cotangent.reshape(frames, width, chans)
     act = jax.nn.silu(x.astype(F32)).astype(BF)
     above, below = neighbours(act)
-    pre = matmul(taps_of(side_pad(jnp.stack([above, act, below], axis=1)), width), fetch(spatial_weight))
+    pre = matmul(taps_of(side_pad(jnp.stack([above, act, below], axis=1)), width), spatial_weight)
     pre = pre.reshape(frames, width, chans)
     bact = jax.nn.silu(pre).astype(BF)
     bext = jnp.concatenate([shift(bact, "tm", 1), bact], axis=0)

time: 199 us -> 201 us (1.010)
  starting transfers between devices: 54.8 us -> 57.6 us
    all_to_all x1, starting transfers between devices: 8.7 us -> 11.4 us  [per_device(): items = lax.all_to_all(items, 'space', 0, 0, tiled=True)]
  transfers between devices with their start and end apart: 19 -> 19, of which waited for: 7 -> 9; matrix products, arithmetic and copies ran while one was open for 3% -> 3% of each run, Pallas kernels for 36% -> 35%
where the time goes in v3:
time: 201 us; the launch traced here: 200 us
  Pallas kernels  78.8 us (39%)
  starting transfers between devices  57.6 us (29%)
  waiting for transfers between devices  45 us (22%)
  local copies, waits for them, and re-layouts  10.6 us (5%)
  matrix products  4.29 us (2%)
  other arithmetic  2.71 us (1%)
    pallas_call x1, Pallas kernels, attn(): pl.pallas_call(functools.partial(attn_kernel, 1.0 / math.sqrt(32), tq, ck...  48.2 us
    ppermute x6, starting transfers between devices, shift(): return lax.ppermute(x, axis, pairs)  16.8 us
    all_to_all x1, waiting for transfers between devices, per_device(): terms = lax.all_to_all(terms, ('tm', 'space'), 0, 0, tiled=True)  12.1 us
    all_to_all x1, waiting for transfers between devices, per_device(): outs = lax.all_to_all(outs, 'space', 0, 0, tiled=True)  11.7 us
    all_to_all x1, starting transfers between devices, per_device(): items = lax.all_to_all(items, 'space', 0, 0, tiled=True)  11.4 us
    all_to_all x1, starting transfers between devices, per_device(): terms = lax.all_to_all(terms, ('tm', 'space'), 0, 0, tiled=True)  10.6 us
    all_to_all x1, waiting for transfers between devices, per_device(): items = lax.all_to_all(items, 'space', 0, 0, tiled=True)  8.7 us
    all_to_all x2, starting transfers between devices, exchange(): lax.all_to_all(x, 'space', 0, 0, axis_index_groups=groups, tiled=True)  8.23 us
  transfers between devices with their start and end apart: 19, of which 9 were waited for; matrix products, arithmetic and copies ran while one was open for 3% of the time, Pallas kernels for 35%

profile of v3, /device:TPU:1, one launch (start us, length us, event | category | flops | bytes accessed | tf_op | source)
XLA Modules:
  0.0 200.0 jit_solution(12140686497395379898)
XLA Ops:
  1.8 3.3 %collective-permute-start.1 = (bf16[2,120,512]{2,1,0:T(8,128)(2,1)S(1)}, bf16[2,120,512]{2,1,0:T(8,128)(2,1)S(1)}, u32[]{:S(2)}, u32[]{:S(2)}) collective-permute-start(bf16[2,120,512]{2,1,0:T(8,128)(2,1)S(1)} %fusion.11.act_ref), channel_id=1, source_target_pairs={{1,0},{2,1},{3,2},{4,3},{5,4},{6,5},{7,6},{8,7},{9,8},{10,9},{11,1... | collective-permute-start | bytes 737288 | tf_op jit(solution)/shard_map/ppermute | solution.py:561
  5.1 3.1 %collective-permute-start = (bf16[2,120,512]{2,1,0:T(8,128)(2,1)S(1)}, bf16[2,120,512]{2,1,0:T(8,128)(2,1)S(1)}, u32[]{:S(2)}, u32[]{:S(2)}) collective-permute-start(bf16[2,120,512]{2,1,0:T(8,128)(2,1)S(1)} %fusion.11.act_ref), channel_id=1, source_target_pairs={{0,1},{1,2},{2,3},{3,4},{4,5},{5,6},{6,7},{7,8},{8,9},{9,10},{10,1... | collective-permute-start | bytes 737288 | tf_op jit(solution)/shard_map/ppermute | solution.py:561
  13.9 2.3 %add_multiply_fusion = (f32[2,120,512]{2,1,0:T(8,128)}, bf16[2,120,512]{2,1,0:T(8,128)(2,1)S(1)}) fusion(bf16[2,120,4608]{2,1,0:T(8,128)(2,1)S(1)} %fusion.17, bf16[4608,512]{1,0:T(8,128)(2,1)S(1)} %copy-done.9), kind=kOutput, calls=%fused_computation.25 | convolution fusion | flops 1133568000 | bytes 7667712 | tf_op jit(solution)/shard_map/dot_general | solution.py:555
  16.2 3.6 %collective-permute-start.2 = (bf16[2,120,512]{2,1,0:T(8,128)(2,1)S(1)}, bf16[2,120,512]{2,1,0:T(8,128)(2,1)S(1)}, u32[]{:S(2)}, u32[]{:S(2)}) collective-permute-start(bf16[2,120,512]{2,1,0:T(8,128)(2,1)S(1)} %get-tuple-element.83), channel_id=1, source_target_pairs={{0,32},{32,64},{64,96},{1,33},{33,65},{65,97},{2,34},{34,66},{66,9... | collective-permute-start | bytes 737288 | tf_op jit(solution)/shard_map/ppermute | solution.py:561
  19.8 3.6 %collective-permute-done.2 = bf16[2,120,512]{2,1,0:T(8,128)(2,1)S(1)} collective-permute-done((bf16[2,120,512]{2,1,0:T(8,128)(2,1)S(1)}, bf16[2,120,512]{2,1,0:T(8,128)(2,1)S(1)}, u32[]{:S(2)}, u32[]{:S(2)}) %collective-permute-start.2) | collective-permute-done | bytes 245792 | tf_op jit(solution)/shard_map/ppermute | solution.py:561
  23.5 2.9 %shard_map.85 = (f32[2,120,512]{2,1,0:T(8,128)}, bf16[2,120,512]{2,1,0:T(8,128)(2,1)S(1)}, bf16[2,16,120,128]{3,2,1,0:T(8,128)(2,1)}) custom-call(bf16[2,120,512]{2,1,0:T(8,128)(2,1)S(1)} %bitcast.68, bf16[4,120,512]{2,1,0:T(8,128)(2,1)S(1)} %pad_maximum_fusion.bext_ref.refs_2_, bf16[2,120,512]{2,1,0:T(8,128)(2,1)S(1)} %bitcast.72, ...), custom_call_target="tpu_custom_call" | custom-call | flops 2000000000 | bytes 6291456 | tf_op jit(solution)/shard_map/pallas_call | solution.py:42
  26.4 11.4 %all-to-all-start = ((bf16[32,120,128]{2,1,0:T(8,128)(2,1)}), bf16[32,120,128]{2,1,0:T(8,128)(2,1)S(1)}, u32[]{:S(2)}, u32[]{:S(2)}) async-start(bf16[32,120,128]{2,1,0:T(8,128)(2,1)} %bitcast.17), calls=%async_computation | async-start | bytes 1966080 | tf_op jit(solution)/shard_map/all_to_all | solution.py:620
  45.5 8.7 %all-to-all-done = bf16[32,120,128]{2,1,0:T(8,128)(2,1)S(1)} async-done(((bf16[32,120,128]{2,1,0:T(8,128)(2,1)}), bf16[32,120,128]{2,1,0:T(8,128)(2,1)S(1)}, u32[]{:S(2)}, u32[]{:S(2)}) %all-to-all-start) | async-done | bytes 983072 | tf_op jit(solution)/shard_map/all_to_all | solution.py:620
  54.2 3.9 %all-to-all-start.1 = ((bf16[8,4,120,256]{3,2,1,0:T(8,128)(2,1)}), bf16[8,4,120,256]{3,2,1,0:T(8,128)(2,1)S(1)}, u32[]{:S(2)}, u32[]{:S(2)}) async-start(bf16[8,4,120,256]{3,2,1,0:T(8,128)(2,1)} %shard_map.86), calls=%async_computation.1 | async-start | bytes 3932160 | tf_op jit(solution)/shard_map/all_to_all | solution.py:576
  58.1 48.2 %shard_map.87 = bf16[3840,128]{1,0:T(8,128)(2,1)} custom-call(bf16[3840,128]{1,0:T(8,128)(2,1)S(1)} %bitcast.70), custom_call_target="tpu_custom_call" | custom-call | flops 22649241600 | bytes 1966080 | tf_op jit(solution)/shard_map/pallas_call | solution.py:212
  106.3 5.2 %all-to-all-start.2 = ((bf16[32,120,128]{2,1,0:T(8,128)(2,1)}), bf16[32,120,128]{2,1,0:T(8,128)(2,1)S(1)}, u32[]{:S(2)}, u32[]{:S(2)}) async-start(bf16[32,120,128]{2,1,0:T(8,128)(2,1)} %bitcast.76), calls=%async_computation.2 | async-start | bytes 1966080 | tf_op jit(solution)/shard_map/all_to_all | solution.py:630
  111.6 3.1 %shard_map.88.at_ref = bf16[3,2,256,1280]{3,2,1,0:T(8,128)(2,1)} custom-call(bf16[8,4,120,256]{3,2,1,0:T(8,128)(2,1)S(1)} %all-to-all-done.1.r_ref), custom_call_target="tpu_custom_call" | custom-call | flops 1000000000 | bytes 6291456 | tf_op jit(solution)/shard_map/pallas_call | solution.py:281
  116.4 11.7 %all-to-all-done.2 = bf16[32,120,128]{2,1,0:T(8,128)(2,1)S(1)} async-done(((bf16[32,120,128]{2,1,0:T(8,128)(2,1)}), bf16[32,120,128]{2,1,0:T(8,128)(2,1)S(1)}, u32[]{:S(2)}, u32[]{:S(2)}) %all-to-all-start.2) | async-done | bytes 983072 | tf_op jit(solution)/shard_map/all_to_all | solution.py:630
  128.0 4.3 %shard_map.90 = (bf16[2,120,512]{2,1,0:T(8,128)(2,1)S(1)}, f32[2,120,512]{2,1,0:T(8,128)}, bf16[2,120,512]{2,1,0:T(8,128)(2,1)S(1)}, bf16[2,120,1024]{2,1,0:T(8,128)(2,1)}, bf16[2,120,1024]{2,1,0:T(8,128)(2,1)S(1)}) custom-call(s32[1]{0:T(128)} %bitcast.14.core_ref, bf16[2,16,120,128]{3,2,1,0:T(8,128)(2,1)S(1)} %bitcast.71, ...), custom_call_target="tpu_custom_call" | custom-call | flops 1000000000 | bytes 6291456 | tf_op jit(solution)/shard_map/pallas_call | solution.py:103
  134.7 4.5 %shard_map.91 = (bf16[56,16,256]{2,1,0:T(8,128)(2,1)}, bf16[56,16,256]{2,1,0:T(8,128)(2,1)S(1)}, bf16[56,16,256]{2,1,0:T(8,128)(2,1)}, bf16[56,16,256]{2,1,0:T(8,128)(2,1)S(1)}) custom-call(s32[1]{0:T(128)} %bitcast.23.line_ref, bf16[2,120,512]{2,1,0:T(8,128)(2,1)S(1)} %get-tuple-element.55.a0_ref, bf16[2,120,512]{2,1,0:T(8,128)(2,1)S(1)} %collective-permute-done.7.a1_ref, ...), custom_call_target="tpu_custom_call" | custom-call | flops 2000000000 | bytes 10485760 | tf_op jit(solution)/shard_map/pallas_call | solution.py:366
  140.4 2.6 %collective-permute-start.11 = (bf16[56,16,256]{2,1,0:T(8,128)(2,1)S(1)}, bf16[56,16,256]{2,1,0:T(8,128)(2,1)}, u32[]{:S(2)}, u32[]{:S(2)}) collective-permute-start(bf16[56,16,256]{2,1,0:T(8,128)(2,1)S(1)} %get-tuple-element.72), channel_id=1, source_target_pairs={{0,24},{1,25},{2,26},{3,27},{4,28},{5,29},{6,30},{7,31},{8,0},{9,1... | collective-permute-start | bytes 1376264 | tf_op jit(solution)/shard_map/ppermute | solution.py:581
  145.0 4.3 %all-to-all-start.3 = ((bf16[8,2,120,128]{3,2,1,0:T(8,128)(2,1)}), bf16[8,2,120,128]{3,2,1,0:T(8,128)(2,1)S(1)}, u32[]{:S(2)}, u32[]{:S(2)}) async-start(bf16[8,2,120,128]{3,2,1,0:T(8,128)(2,1)} %get-tuple-element.66), calls=%async_computation.3 | async-start | bytes 983040 | tf_op jit(solution)/shard_map/all_to_all | solution.py:576
  151.4 3.5 %collective-permute-start.12 = (bf16[2,120,512]{2,1,0:T(8,128)(2,1)}, bf16[2,120,512]{2,1,0:T(8,128)(2,1)S(1)}, u32[]{:S(2)}, u32[]{:S(2)}) collective-permute-start(bf16[2,120,512]{2,1,0:T(8,128)(2,1)} %get-tuple-element.74.mid_ref), channel_id=1, source_target_pairs={{0,1},{1,2},{2,3},{3,4},{4,5},{5,6},{6,7},{7,8},{8,9},{9,10},{10,1... | collective-permute-start | bytes 737288 | tf_op jit(solution)/shard_map/ppermute | solution.py:561
  158.5 4.9 %collective-permute-done.10.refs_1_ = bf16[56,16,256]{2,1,0:T(8,128)(2,1)} collective-permute-done((bf16[56,16,256]{2,1,0:T(8,128)(2,1)S(1)}, bf16[56,16,256]{2,1,0:T(8,128)(2,1)}, u32[]{:S(2)}, u32[]{:S(2)}) %collective-permute-start.10) | collective-permute-done | bytes 458784 | tf_op jit(solution)/shard_map/ppermute | solution.py:581
  163.4 5.8 %shard_map.93 = bf16[128,32,128]{2,1,0:T(8,128)(2,1)} custom-call(bf16[3,2,256,1280]{3,2,1,0:T(8,128)(2,1)} %shard_map.88.at_ref, bf16[8,2,120,128]{3,2,1,0:T(8,128)(2,1)} %copy-done.20, bf16[56,16,256]{2,1,0:T(8,128)(2,1)} %collective-permute-done.9.refs_0_, bf16[56,16,256]{2,1,0:T(8,128)(2,1)} %collective-permute-done.10.refs_1_, ...), custom_call_target="tpu_custom_call" | custom-call | flops 2000000000 | bytes 10485760 | tf_op jit(solution)/shard_map/pallas_call | solution.py:433
  169.2 10.6 %all-to-all-start.4 = ((bf16[128,32,128]{2,1,0:T(8,128)(2,1)}), bf16[128,32,128]{2,1,0:T(8,128)(2,1)S(1)}, u32[]{:S(2)}, u32[]{:S(2)}) async-start(bf16[128,32,128]{2,1,0:T(8,128)(2,1)} %shard_map.93), calls=%async_computation.4 | async-start | bytes 2097152 | tf_op jit(solution)/shard_map/all_to_all | solution.py:651
  179.9 2.3 %copy-done.10 = bf16[4608,512]{1,0:T(8,128)(2,1)S(1)} copy-done((bf16[4608,512]{1,0:T(8,128)(2,1)S(1)}, bf16[4608,512]{1,0:T(8,128)(2,1)}, u32[]{:S(2)}) %copy-start.10) | copy-done | bytes 4718616
  183.2 3.9 %shard_map.94 = bf16[2,120,512]{2,1,0:T(8,128)(2,1)} custom-call(bf16[2,120,512]{2,1,0:T(8,128)(2,1)S(1)} %copy-done.16, bf16[2,120,512]{2,1,0:T(8,128)(2,1)S(1)} %collective-permute-done.12.above_ref, bf16[2,120,512]{2,1,0:T(8,128)(2,1)S(1)} %collective-permute-done.13.below_ref, f32[2,120,512]{2,1,0:T(8,128)S(1)} %copy-done.19, ...), custom_call_target="tpu_custom_call" | custom-call | flops 2000000000 | bytes 8388608 | tf_op jit(solution)/shard_map/pallas_call | solution.py:541
  187.1 12.1 %all-to-all-done.4.terms_ref = bf16[128,32,128]{2,1,0:T(8,128)(2,1)S(1)} async-done(((bf16[128,32,128]{2,1,0:T(8,128)(2,1)}), bf16[128,32,128]{2,1,0:T(8,128)(2,1)S(1)}, u32[]{:S(2)}, u32[]{:S(2)}) %all-to-all-start.4) | async-done | bytes 1048608 | tf_op jit(solution)/shard_map/all_to_all | solution.py:651
  (88 shorter events, 29.2 us)
Async XLA Ops:
  0.6 11.1 %copy-start = (bf16[2,1,120,512]{3,2,1,0:T(8,128)(2,1)S(1)}, bf16[2,1,120,512]{3,2,1,0:T(8,128)(2,1)}, u32[]{:S(2)}) copy-start(bf16[2,1,120,512]{3,2,1,0:T(8,128)(2,1)} %param.6) | copy-start | bytes 737284
  1.8 8.4 %collective-permute-start.1 = (bf16[2,120,512]{2,1,0:T(8,128)(2,1)S(1)}, bf16[2,120,512]{2,1,0:T(8,128)(2,1)S(1)}, u32[]{:S(2)}, u32[]{:S(2)}) collective-permute-start(bf16[2,120,512]{2,1,0:T(8,128)(2,1)S(1)} %fusion.11.act_ref), channel_id=1, source_target_pairs={{1,0},{2,1},{3,2},{4,3},{5,4},{6,5},{7,6},{8,7},{9,8},{10,9},{11,1... | collective-permute-start | bytes 737288 | tf_op jit(solution)/shard_map/ppermute | solution.py:561
  5.1 6.2 %collective-permute-start = (bf16[2,120,512]{2,1,0:T(8,128)(2,1)S(1)}, bf16[2,120,512]{2,1,0:T(8,128)(2,1)S(1)}, u32[]{:S(2)}, u32[]{:S(2)}) collective-permute-start(bf16[2,120,512]{2,1,0:T(8,128)(2,1)S(1)} %fusion.11.act_ref), channel_id=1, source_target_pairs={{0,1},{1,2},{2,3},{3,4},{4,5},{5,6},{6,7},{7,8},{8,9},{9,10},{10,1... | collective-permute-start | bytes 737288 | tf_op jit(solution)/shard_map/ppermute | solution.py:561
  16.2 7.2 %collective-permute-start.2 = (bf16[2,120,512]{2,1,0:T(8,128)(2,1)S(1)}, bf16[2,120,512]{2,1,0:T(8,128)(2,1)S(1)}, u32[]{:S(2)}, u32[]{:S(2)}) collective-permute-start(bf16[2,120,512]{2,1,0:T(8,128)(2,1)S(1)} %get-tuple-element.83), channel_id=1, source_target_pairs={{0,32},{32,64},{64,96},{1,33},{33,65},{65,97},{2,34},{34,66},{66,9... | collective-permute-start | bytes 737288 | tf_op jit(solution)/shard_map/ppermute | solution.py:561
  23.4 14.3 %copy-start.6 = (bf16[4,120,512]{2,1,0:T(8,128)(2,1)}, bf16[4,120,512]{2,1,0:T(8,128)(2,1)S(1)}, u32[]{:S(2)}) copy-start(bf16[4,120,512]{2,1,0:T(8,128)(2,1)S(1)} %pad_maximum_fusion.bext_ref.refs_2_) | copy-start | bytes 1474564
  26.4 17.1 %copy-start.14 = (bf16[2,120,512]{2,1,0:T(8,128)(2,1)}, bf16[2,120,512]{2,1,0:T(8,128)(2,1)S(1)}, u32[]{:S(2)}) copy-start(bf16[2,120,512]{2,1,0:T(8,128)(2,1)S(1)} %get-tuple-element.42.refs_0_) | copy-start | bytes 737284
  26.4 27.9 %all-to-all-start = ((bf16[32,120,128]{2,1,0:T(8,128)(2,1)}), bf16[32,120,128]{2,1,0:T(8,128)(2,1)S(1)}, u32[]{:S(2)}, u32[]{:S(2)}) async-start(bf16[32,120,128]{2,1,0:T(8,128)(2,1)} %bitcast.17), calls=%async_computation | async-start | bytes 1966080 | tf_op jit(solution)/shard_map/all_to_all | solution.py:620
  37.8 7.0 %collective-permute-start.5 = (bf16[4,120,512]{2,1,0:T(8,128)(2,1)S(1)}, bf16[4,120,512]{2,1,0:T(8,128)(2,1)S(1)}, u32[]{:S(2)}, u32[]{:S(2)}) collective-permute-start(bf16[4,120,512]{2,1,0:T(8,128)(2,1)S(1)} %pad_maximum_fusion.bext_ref.refs_2_), channel_id=1, source_target_pairs={{0,1},{1,0},{2,3},{3,2},{4,5},{5,4},{6,7},{7,6},{8,9},{9,8},{10,11... | collective-permute-start | bytes 1474568 | tf_op jit(solution)/shard_map/ppermute | solution.py:566
  38.9 4.6 %collective-permute-start.4 = (bf16[2,120,512]{2,1,0:T(8,128)(2,1)S(1)}, bf16[2,120,512]{2,1,0:T(8,128)(2,1)S(1)}, u32[]{:S(2)}, u32[]{:S(2)}) collective-permute-start(bf16[2,120,512]{2,1,0:T(8,128)(2,1)S(1)} %get-tuple-element.42.refs_0_), channel_id=1, source_target_pairs={{0,1},{1,0},{2,3},{3,2},{4,5},{5,4},{6,7},{7,6},{8,9},{9,8},{10,11... | collective-permute-start | bytes 737288 | tf_op jit(solution)/shard_map/ppermute | solution.py:566
  40.7 2.7 %collective-permute-start.3 = (bf16[2,120,256]{2,1,0:T(8,128)(2,1)S(1)}, bf16[2,120,256]{2,1,0:T(8,128)(2,1)S(1)}, u32[]{:S(2)}, u32[]{:S(2)}) collective-permute-start(bf16[2,120,256]{2,1,0:T(8,128)(2,1)S(1)} %bitcast.80), channel_id=1, source_target_pairs={{0,1},{1,0},{2,3},{3,2},{4,5},{5,4},{6,7},{7,6},{8,9},{9,8},{10,11... | collective-permute-start | bytes 368648 | tf_op jit(solution)/shard_map/ppermute | solution.py:566
  54.2 52.1 %all-to-all-start.1 = ((bf16[8,4,120,256]{3,2,1,0:T(8,128)(2,1)}), bf16[8,4,120,256]{3,2,1,0:T(8,128)(2,1)S(1)}, u32[]{:S(2)}, u32[]{:S(2)}) async-start(bf16[8,4,120,256]{3,2,1,0:T(8,128)(2,1)} %shard_map.86), calls=%async_computation.1 | async-start | bytes 3932160 | tf_op jit(solution)/shard_map/all_to_all | solution.py:576
  106.3 21.7 %all-to-all-start.2 = ((bf16[32,120,128]{2,1,0:T(8,128)(2,1)}), bf16[32,120,128]{2,1,0:T(8,128)(2,1)S(1)}, u32[]{:S(2)}, u32[]{:S(2)}) async-start(bf16[32,120,128]{2,1,0:T(8,128)(2,1)} %bitcast.76), calls=%async_computation.2 | async-start | bytes 1966080 | tf_op jit(solution)/shard_map/all_to_all | solution.py:630
  132.4 2.3 %collective-permute-start.8 = (bf16[2,120,1024]{2,1,0:T(8,128)(2,1)S(1)}, bf16[2,120,1024]{2,1,0:T(8,128)(2,1)S(1)}, u32[]{:S(2)}, u32[]{:S(2)}) collective-permute-start(bf16[2,120,1024]{2,1,0:T(8,128)(2,1)S(1)} %get-tuple-element.58), channel_id=1, source_target_pairs={{0,1},{1,0},{2,3},{3,2},{4,5},{5,4},{6,7},{7,6},{8,9},{9,8},{10,11... | collective-permute-start | bytes 1474568 | tf_op jit(solution)/shard_map/ppermute | solution.py:566
  132.9 1.8 collective-permute-start.7
  133.0 10.0 %collective-permute-start.6 = (bf16[2,120,512]{2,1,0:T(8,128)(2,1)S(1)}, bf16[2,120,512]{2,1,0:T(8,128)(2,1)S(1)}, u32[]{:S(2)}, u32[]{:S(2)}) collective-permute-start(bf16[2,120,512]{2,1,0:T(8,128)(2,1)S(1)} %get-tuple-element.56.own_ref), channel_id=1, source_target_pairs={{32,0},{64,32},{96,64},{33,1},{65,33},{97,65},{34,2},{66,34},{98,6... | collective-permute-start | bytes 737288 | tf_op jit(solution)/shard_map/ppermute | solution.py:561
  139.2 15.7 %copy-start.4 = (bf16[512,512]{1,0:T(8,128)(2,1)S(1)}, bf16[512,512]{1,0:T(8,128)(2,1)}, u32[]{:S(2)}) copy-start(bf16[512,512]{1,0:T(8,128)(2,1)} %ow_ref.1) | copy-start | bytes 1572868
  139.2 19.3 %collective-permute-start.9 = (bf16[56,16,256]{2,1,0:T(8,128)(2,1)}, bf16[56,16,256]{2,1,0:T(8,128)(2,1)}, u32[]{:S(2)}, u32[]{:S(2)}) collective-permute-start(bf16[56,16,256]{2,1,0:T(8,128)(2,1)} %get-tuple-element.70), channel_id=1, source_target_pairs={{0,16},{1,17},{2,18},{3,19},{4,20},{5,21},{6,22},{7,23},{8,24},{9,... | collective-permute-start | bytes 1376264 | tf_op jit(solution)/shard_map/ppermute | solution.py:581
  140.3 23.1 %collective-permute-start.10 = (bf16[56,16,256]{2,1,0:T(8,128)(2,1)S(1)}, bf16[56,16,256]{2,1,0:T(8,128)(2,1)}, u32[]{:S(2)}, u32[]{:S(2)}) collective-permute-start(bf16[56,16,256]{2,1,0:T(8,128)(2,1)S(1)} %get-tuple-element.71), channel_id=1, source_target_pairs={{0,8},{1,9},{2,10},{3,11},{4,12},{5,13},{6,14},{7,15},{8,16},{9,17... | collective-permute-start | bytes 1376264 | tf_op jit(solution)/shard_map/ppermute | solution.py:581
  140.4 23.0 %collective-permute-start.11 = (bf16[56,16,256]{2,1,0:T(8,128)(2,1)S(1)}, bf16[56,16,256]{2,1,0:T(8,128)(2,1)}, u32[]{:S(2)}, u32[]{:S(2)}) collective-permute-start(bf16[56,16,256]{2,1,0:T(8,128)(2,1)S(1)} %get-tuple-element.72), channel_id=1, source_target_pairs={{0,24},{1,25},{2,26},{3,27},{4,28},{5,29},{6,30},{7,31},{8,0},{9,1... | collective-permute-start | bytes 1376264 | tf_op jit(solution)/shard_map/ppermute | solution.py:581
  145.0 13.5 %all-to-all-start.3 = ((bf16[8,2,120,128]{3,2,1,0:T(8,128)(2,1)}), bf16[8,2,120,128]{3,2,1,0:T(8,128)(2,1)S(1)}, u32[]{:S(2)}, u32[]{:S(2)}) async-start(bf16[8,2,120,128]{3,2,1,0:T(8,128)(2,1)} %get-tuple-element.66), calls=%async_computation.3 | async-start | bytes 983040 | tf_op jit(solution)/shard_map/all_to_all | solution.py:576
  149.4 19.8 %collective-permute-start.13 = (bf16[2,120,512]{2,1,0:T(8,128)(2,1)}, bf16[2,120,512]{2,1,0:T(8,128)(2,1)S(1)}, u32[]{:S(2)}, u32[]{:S(2)}) collective-permute-start(bf16[2,120,512]{2,1,0:T(8,128)(2,1)} %get-tuple-element.74.mid_ref), channel_id=1, source_target_pairs={{1,0},{2,1},{3,2},{4,3},{5,4},{6,5},{7,6},{8,7},{9,8},{10,9},{11,1... | collective-permute-start | bytes 737288 | tf_op jit(solution)/shard_map/ppermute | solution.py:561
  151.4 17.8 %collective-permute-start.12 = (bf16[2,120,512]{2,1,0:T(8,128)(2,1)}, bf16[2,120,512]{2,1,0:T(8,128)(2,1)S(1)}, u32[]{:S(2)}, u32[]{:S(2)}) collective-permute-start(bf16[2,120,512]{2,1,0:T(8,128)(2,1)} %get-tuple-element.74.mid_ref), channel_id=1, source_target_pairs={{0,1},{1,2},{2,3},{3,4},{4,5},{5,6},{6,7},{7,8},{8,9},{9,10},{10,1... | collective-permute-start | bytes 737288 | tf_op jit(solution)/shard_map/ppermute | solution.py:561
  158.5 21.3 %copy-start.16 = (bf16[2,120,512]{2,1,0:T(8,128)(2,1)S(1)}, bf16[2,120,512]{2,1,0:T(8,128)(2,1)}, u32[]{:S(2)}) copy-start(bf16[2,120,512]{2,1,0:T(8,128)(2,1)} %get-tuple-element.74.mid_ref) | copy-start | bytes 737284
  169.2 30.0 %all-to-all-start.4 = ((bf16[128,32,128]{2,1,0:T(8,128)(2,1)}), bf16[128,32,128]{2,1,0:T(8,128)(2,1)S(1)}, u32[]{:S(2)}, u32[]{:S(2)}) async-start(bf16[128,32,128]{2,1,0:T(8,128)(2,1)} %shard_map.93), calls=%async_computation.4 | async-start | bytes 2097152 | tf_op jit(solution)/shard_map/all_to_all | solution.py:651
  (17 other events, 80.0 us)
